TPU v7x, 32 devices: a whole 2x2x4 slice. The times are simulated.
32 devices in a mesh: dp: 8 (over z, x), seq: 4 (over y, core).
Axes of the slice: x: 2, y: 2, z: 4, core: 2. Of those that a mesh axis runs over, the one named last changes fastest.
Arguments:
- dec_states: bfloat16 [8, 1024, 768], P('dp', 'seq'), may hold values from -6 to 6
- enc_states: bfloat16 [8, 1024, 768], P('dp', 'seq'), may hold values from -6 to 6
- out_grad: bfloat16 [8, 1024, 768], P('dp', 'seq'), may hold values from -6 to 6
- dec_lengths: int32 [8, 4], P('dp'), may hold values from 1 to 1021, as said below
- enc_lengths: int32 [8, 4], P('dp'), may hold values from 1 to 1021, as said below
- self_query: bfloat16 [768, 768], replicated, may hold values from -0.109375 to 0.109375
- self_key: bfloat16 [768, 768], replicated, may hold values from -0.109375 to 0.109375
- self_value: bfloat16 [768, 768], replicated, may hold values from -0.21875 to 0.21875
- self_output: bfloat16 [768, 768], replicated, may hold values from -1.25 to 1.25
- cross_query: bfloat16 [768, 768], replicated, may hold values from -0.109375 to 0.109375
- cross_key: bfloat16 [768, 768], replicated, may hold values from -0.109375 to 0.109375
- cross_value: bfloat16 [768, 768], replicated, may hold values from -0.21875 to 0.21875
- cross_output: bfloat16 [768, 768], replicated, may hold values from -1.25 to 1.25
- ffn_in: bfloat16 [768, 3072], replicated, may hold values from -0.21875 to 0.21875
- ffn_out: bfloat16 [3072, 768], replicated, may hold values from -0.109375 to 0.109375
- gain_self: bfloat16 [768], replicated, may hold values from 0.099609375 to 1.8984375
- gain_cross: bfloat16 [768], replicated, may hold values from 0.099609375 to 1.8984375
- gain_ffn: bfloat16 [768], replicated, may hold values from 0.099609375 to 1.8984375
- position_bias: bfloat16 [32, 12], replicated, may hold values from -4 to 4
Outputs:
- layer_out: bfloat16 [8, 1024, 768], P('dp', 'seq')
- dec_grad: float32 [8, 1024, 768], P('dp', 'seq')
- enc_grad: float32 [8, 1024, 768], P('dp', 'seq')
- grad_self_query: float32 [768, 768], P('seq')
- grad_self_key: float32 [768, 768], P('seq')
- grad_self_value: float32 [768, 768], P('seq')
- grad_self_output: float32 [768, 768], P('seq')
- grad_cross_query: float32 [768, 768], P('seq')
- grad_cross_key: float32 [768, 768], P('seq')
- grad_cross_value: float32 [768, 768], P('seq')
- grad_cross_output: float32 [768, 768], P('seq')
- grad_ffn_in: float32 [768, 3072], P('seq')
- grad_ffn_out: float32 [3072, 768], P('seq')
- grad_gain_self: float32 [768], P('seq')
- grad_gain_cross: float32 [768], P('seq')
- grad_gain_ffn: float32 [768], P('seq')
- grad_position_bias: float32 [32, 12], P('seq')
Inputs may be any that keep to these rules, and one draw needn't show every extreme that they name: `dec_lengths`: the 4 lengths of a row sum to 1024. In every row one item, the second or third, begins within the first 256 positions and ends within the last 256; each other item is shorter than 128. In one row of every draw the other items have length 1 each. `enc_lengths`: as for dec_lengths, drawn apart from them.
All inputs are finite; a program needn't handle non-finite values.
Results may differ from a plain program's by a relative error of at most 0.028.
The roundings to bfloat16 on the way count: a program that leaves them out, or rounds other values in their place, can miss the bound.
Values may be sent and summed in bfloat16 or wider, within the bound.
A program may use at most 192 MiB of HBM per device.

v0:
```python
import math

import jax
import jax.numpy as jnp
from jax import lax
from jax.sharding import PartitionSpec as P

EPS = 1e-06
NEG = -1000000000.0


def bucket_of(distance):
    farther = jnp.full(distance.shape, 16, jnp.int32)
    for level in range(1, 16):
        farther = farther + (distance >= math.ceil(16 * 8 ** (level / 16))).astype(jnp.int32)
    return jnp.where(distance < 16, distance, farther)


def item_ids(lengths, count):
    starts = jnp.cumsum(lengths) - lengths
    places = jnp.arange(count, dtype=jnp.int32)
    return jnp.sum((places[:, None] >= starts[None, :]).astype(jnp.int32), axis=1) - 1


def norm_rows(values, gain):
    return values * lax.rsqrt(jnp.mean(values * values, axis=-1, keepdims=True) + EPS) * gain


def matmul(left, right):
    return jnp.dot(left, right, preferred_element_type=jnp.float32)


def matmul_right_t(left, right):
    return lax.dot_general(
        left, right, (((1,), (1,)), ((), ())), preferred_element_type=jnp.float32
    )


def matmul_left_t(left, right):
    return lax.dot_general(
        left, right, (((0,), (0,)), ((), ())), preferred_element_type=jnp.float32
    )


def block_scores(query_heads, keys_all, start, span, allowed, position_terms, table):
    heads, head_dim = (query_heads.shape[1], query_heads.shape[2])
    key_block = keys_all[start : start + span].reshape(span, heads, head_dim)
    raw = jnp.einsum("shd,khd->hsk", query_heads, key_block, preferred_element_type=jnp.float32)
    if table is not None:
        raw = raw + jnp.einsum(
            "skb,bh->hsk", position_terms(start, span), table, preferred_element_type=jnp.float32
        )
    return (jnp.where(allowed(start, span)[None], raw, NEG), key_block)


def attention_forward(queries, keys_all, values_all, allowed, position_terms, table, heads):
    count, width = queries.shape
    total = keys_all.shape[0]
    span = min(512, total)
    head_dim = width // heads
    query_heads = queries.reshape(count, heads, head_dim)
    running = jnp.full((heads, count), -jnp.inf, jnp.float32)
    mass = jnp.zeros((heads, count), jnp.float32)
    for start in range(0, total, span):
        scores, _ = block_scores(query_heads, keys_all, start, span, allowed, position_terms, table)
        newer = jnp.maximum(running, jnp.max(scores, axis=2))
        mass = mass * jnp.exp(running - newer) + jnp.sum(
            jnp.exp(scores - newer[:, :, None]), axis=2
        )
        running = newer
    log_mass = running + jnp.log(mass)
    context = jnp.zeros((count, heads, head_dim), jnp.float32)
    for start in range(0, total, span):
        scores, _ = block_scores(query_heads, keys_all, start, span, allowed, position_terms, table)
        probs = jnp.exp(scores - log_mass[:, :, None]).astype(jnp.bfloat16)
        value_block = values_all[start : start + span].reshape(span, heads, head_dim)
        context = context + jnp.einsum(
            "hsk,khd->shd", probs, value_block, preferred_element_type=jnp.float32
        )
    return (context.reshape(count, width), log_mass)


def attention_backward(
    queries,
    keys_all,
    values_all,
    allowed,
    position_terms,
    table,
    heads,
    context,
    log_mass,
    context_grad,
):
    count, width = queries.shape
    total = keys_all.shape[0]
    span = min(512, total)
    head_dim = width // heads
    query_heads = queries.reshape(count, heads, head_dim)
    grad_heads = context_grad.reshape(count, heads, head_dim)
    row_terms = jnp.sum(
        grad_heads.astype(jnp.float32) * context.reshape(count, heads, head_dim), axis=2
    ).T
    query_grad = jnp.zeros((count, heads, head_dim), jnp.float32)
    key_parts = []
    value_parts = []
    table_grad = None
    if table is not None:
        table_grad = jnp.zeros(table.shape, jnp.float32)
    for start in range(0, total, span):
        scores, key_block = block_scores(
            query_heads, keys_all, start, span, allowed, position_terms, table
        )
        value_block = values_all[start : start + span].reshape(span, heads, head_dim)
        probs = jnp.exp(scores - log_mass[:, :, None])
        prob_grad = jnp.einsum(
            "shd,khd->hsk", grad_heads, value_block, preferred_element_type=jnp.float32
        )
        score_grad = (probs * (prob_grad - row_terms[:, :, None])).astype(jnp.bfloat16)
        query_grad = query_grad + jnp.einsum(
            "hsk,khd->shd", score_grad, key_block, preferred_element_type=jnp.float32
        )
        key_parts.append(
            jnp.einsum(
                "hsk,shd->khd", score_grad, query_heads, preferred_element_type=jnp.float32
            ).reshape(span, width)
        )
        value_parts.append(
            jnp.einsum(
                "hsk,shd->khd",
                probs.astype(jnp.bfloat16),
                grad_heads,
                preferred_element_type=jnp.float32,
            ).reshape(span, width)
        )
        if table is not None:
            table_grad = table_grad + jnp.einsum(
                "hsk,skb->bh",
                score_grad,
                position_terms(start, span),
                preferred_element_type=jnp.float32,
            )
    return (
        query_grad.reshape(count, width),
        jnp.concatenate(key_parts, axis=0),
        jnp.concatenate(value_parts, axis=0),
        table_grad,
    )


def on_device(
    dec_states,
    enc_states,
    out_grad,
    dec_lengths,
    enc_lengths,
    self_query,
    self_key,
    self_value,
    self_output,
    cross_query,
    cross_key,
    cross_value,
    cross_output,
    ffn_in,
    ffn_out,
    gain_self,
    gain_cross,
    gain_ffn,
    position_bias,
):
    count = dec_states.shape[1]
    heads = position_bias.shape[1]
    total = count * lax.axis_size("seq")
    first_place = lax.axis_index("seq") * count
    own_places = first_place + jnp.arange(count, dtype=jnp.int32)
    all_places = jnp.arange(total, dtype=jnp.int32)
    dec_items = item_ids(dec_lengths[0], total)
    enc_items = item_ids(enc_lengths[0], total)
    own_items = lax.dynamic_slice_in_dim(dec_items, first_place, count)
    bucket_range = jnp.arange(position_bias.shape[0], dtype=jnp.int32)

    def self_allowed(start, span):
        same = own_items[:, None] == dec_items[start : start + span][None, :]
        return same & (all_places[start : start + span][None, :] <= own_places[:, None])

    def cross_allowed(start, span):
        return own_items[:, None] == enc_items[start : start + span][None, :]

    def position_terms(start, span):
        distance = jnp.maximum(own_places[:, None] - all_places[start : start + span][None, :], 0)
        return (bucket_of(distance)[:, :, None] == bucket_range[None, None, :]).astype(jnp.bfloat16)

    states = dec_states[0].astype(jnp.float32)
    encoded = enc_states[0]
    gain_one = gain_self.astype(jnp.float32)
    gain_two = gain_cross.astype(jnp.float32)
    gain_three = gain_ffn.astype(jnp.float32)
    normed_self = norm_rows(states, gain_one).astype(jnp.bfloat16)
    queries = matmul(normed_self, self_query).astype(jnp.bfloat16)
    keys_own = matmul(normed_self, self_key).astype(jnp.bfloat16)
    values_own = matmul(normed_self, self_value).astype(jnp.bfloat16)
    keys_all, values_all = (
        lax.all_gather(keys_own, "seq", axis=0, tiled=True),
        lax.all_gather(values_own, "seq", axis=0, tiled=True),
    )
    context, self_mass = attention_forward(
        queries, keys_all, values_all, self_allowed, position_terms, position_bias, heads
    )
    context_low = context.astype(jnp.bfloat16)
    first = states + matmul(context_low, self_output)
    normed_cross = norm_rows(first, gain_two).astype(jnp.bfloat16)
    cross_queries = matmul(normed_cross, cross_query).astype(jnp.bfloat16)
    cross_keys_own = matmul(encoded, cross_key).astype(jnp.bfloat16)
    cross_values_own = matmul(encoded, cross_value).astype(jnp.bfloat16)
    cross_keys_all, cross_values_all = (
        lax.all_gather(cross_keys_own, "seq", axis=0, tiled=True),
        lax.all_gather(cross_values_own, "seq", axis=0, tiled=True),
    )
    cross_context, cross_mass = attention_forward(
        cross_queries, cross_keys_all, cross_values_all, cross_allowed, None, None, heads
    )
    cross_low = cross_context.astype(jnp.bfloat16)
    second = first + matmul(cross_low, cross_output)
    normed_ffn = norm_rows(second, gain_three).astype(jnp.bfloat16)
    pre_act = matmul(normed_ffn, ffn_in)
    inner_low = jax.nn.gelu(pre_act, approximate=False).astype(jnp.bfloat16)
    layer_out = (second + matmul(inner_low, ffn_out)).astype(jnp.bfloat16)
    cotangent = out_grad[0].astype(jnp.float32)
    ffn_head_grad = cotangent.astype(jnp.bfloat16)
    grad_ffn_out = matmul_left_t(inner_low, ffn_head_grad)
    inner_grad = matmul_right_t(ffn_head_grad, ffn_out)
    _, gelu_back = jax.vjp(lambda values: jax.nn.gelu(values, approximate=False), pre_act)
    pre_grad = gelu_back(inner_grad)[0].astype(jnp.bfloat16)
    grad_ffn_in = matmul_left_t(normed_ffn, pre_grad)
    _, ffn_norm_back = jax.vjp(norm_rows, second, gain_three)
    second_part, gain_ffn_grad = ffn_norm_back(matmul_right_t(pre_grad, ffn_in))
    second_grad = cotangent + second_part
    cross_head_grad = second_grad.astype(jnp.bfloat16)
    grad_cross_output = matmul_left_t(cross_low, cross_head_grad)
    cross_context_grad = matmul_right_t(cross_head_grad, cross_output).astype(jnp.bfloat16)
    cross_query_grad, cross_key_part, cross_value_part, _ = attention_backward(
        cross_queries,
        cross_keys_all,
        cross_values_all,
        cross_allowed,
        None,
        None,
        heads,
        cross_context,
        cross_mass,
        cross_context_grad,
    )
    cross_key_own, cross_value_own = (
        lax.psum_scatter(
            cross_key_part.astype(jnp.bfloat16), "seq", scatter_dimension=0, tiled=True
        ).astype(jnp.float32),
        lax.psum_scatter(
            cross_value_part.astype(jnp.bfloat16), "seq", scatter_dimension=0, tiled=True
        ).astype(jnp.float32),
    )
    cross_query_low = cross_query_grad.astype(jnp.bfloat16)
    cross_key_low = cross_key_own.astype(jnp.bfloat16)
    cross_value_low = cross_value_own.astype(jnp.bfloat16)
    grad_cross_query = matmul_left_t(normed_cross, cross_query_low)
    grad_cross_key = matmul_left_t(encoded, cross_key_low)
    grad_cross_value = matmul_left_t(encoded, cross_value_low)
    enc_grad = matmul_right_t(cross_key_low, cross_key) + matmul_right_t(
        cross_value_low, cross_value
    )
    _, cross_norm_back = jax.vjp(norm_rows, first, gain_two)
    first_part, gain_cross_grad = cross_norm_back(matmul_right_t(cross_query_low, cross_query))
    first_grad = second_grad + first_part
    self_head_grad = first_grad.astype(jnp.bfloat16)
    grad_self_output = matmul_left_t(context_low, self_head_grad)
    context_grad = matmul_right_t(self_head_grad, self_output).astype(jnp.bfloat16)
    query_grad, key_part, value_part, bias_grad = attention_backward(
        queries,
        keys_all,
        values_all,
        self_allowed,
        position_terms,
        position_bias,
        heads,
        context,
        self_mass,
        context_grad,
    )
    key_own, value_own = (
        lax.psum_scatter(
            key_part.astype(jnp.bfloat16), "seq", scatter_dimension=0, tiled=True
        ).astype(jnp.float32),
        lax.psum_scatter(
            value_part.astype(jnp.bfloat16), "seq", scatter_dimension=0, tiled=True
        ).astype(jnp.float32),
    )
    query_low = query_grad.astype(jnp.bfloat16)
    key_low = key_own.astype(jnp.bfloat16)
    value_low = value_own.astype(jnp.bfloat16)
    grad_self_query = matmul_left_t(normed_self, query_low)
    grad_self_key = matmul_left_t(normed_self, key_low)
    grad_self_value = matmul_left_t(normed_self, value_low)
    normed_grad = (
        matmul_right_t(query_low, self_query)
        + matmul_right_t(key_low, self_key)
        + matmul_right_t(value_low, self_value)
    )
    _, self_norm_back = jax.vjp(norm_rows, states, gain_one)
    state_part, gain_self_grad = self_norm_back(normed_grad)
    dec_grad = first_grad + state_part
    summed = lax.psum(
        (
            lax.psum_scatter(
                grad_self_query.astype(jnp.bfloat16), "seq", scatter_dimension=0, tiled=True
            ).astype(jnp.float32),
            lax.psum_scatter(
                grad_self_key.astype(jnp.bfloat16), "seq", scatter_dimension=0, tiled=True
            ).astype(jnp.float32),
            lax.psum_scatter(
                grad_self_value.astype(jnp.bfloat16), "seq", scatter_dimension=0, tiled=True
            ).astype(jnp.float32),
            lax.psum_scatter(
                grad_self_output.astype(jnp.bfloat16), "seq", scatter_dimension=0, tiled=True
            ).astype(jnp.float32),
            lax.psum_scatter(
                grad_cross_query.astype(jnp.bfloat16), "seq", scatter_dimension=0, tiled=True
            ).astype(jnp.float32),
            lax.psum_scatter(
                grad_cross_key.astype(jnp.bfloat16), "seq", scatter_dimension=0, tiled=True
            ).astype(jnp.float32),
            lax.psum_scatter(
                grad_cross_value.astype(jnp.bfloat16), "seq", scatter_dimension=0, tiled=True
            ).astype(jnp.float32),
            lax.psum_scatter(
                grad_cross_output.astype(jnp.bfloat16), "seq", scatter_dimension=0, tiled=True
            ).astype(jnp.float32),
            lax.psum_scatter(
                grad_ffn_in.astype(jnp.bfloat16), "seq", scatter_dimension=0, tiled=True
            ).astype(jnp.float32),
            lax.psum_scatter(
                grad_ffn_out.astype(jnp.bfloat16), "seq", scatter_dimension=0, tiled=True
            ).astype(jnp.float32),
            lax.psum_scatter(
                gain_self_grad.astype(jnp.bfloat16), "seq", scatter_dimension=0, tiled=True
            ).astype(jnp.float32),
            lax.psum_scatter(
                gain_cross_grad.astype(jnp.bfloat16), "seq", scatter_dimension=0, tiled=True
            ).astype(jnp.float32),
            lax.psum_scatter(
                gain_ffn_grad.astype(jnp.bfloat16), "seq", scatter_dimension=0, tiled=True
            ).astype(jnp.float32),
            lax.psum_scatter(
                bias_grad.astype(jnp.bfloat16), "seq", scatter_dimension=0, tiled=True
            ).astype(jnp.float32),
        ),
        "dp",
    )
    return (
        layer_out[None],
        dec_grad[None],
        enc_grad[None],
        summed[0],
        summed[1],
        summed[2],
        summed[3],
        summed[4],
        summed[5],
        summed[6],
        summed[7],
        summed[8],
        summed[9],
        summed[10],
        summed[11],
        summed[12],
        summed[13],
    )


def solution(mesh):
    return jax.shard_map(
        on_device,
        mesh=mesh,
        in_specs=(
            P("dp", "seq", None),
            P("dp", "seq", None),
            P("dp", "seq", None),
            P("dp", None),
            P("dp", None),
            P(),
            P(),
            P(),
            P(),
            P(),
            P(),
            P(),
            P(),
            P(),
            P(),
            P(),
            P(),
            P(),
            P(),
        ),
        out_specs=(
            P("dp", "seq", None),
            P("dp", "seq", None),
            P("dp", "seq", None),
            P("seq", None),
            P("seq", None),
            P("seq", None),
            P("seq", None),
            P("seq", None),
            P("seq", None),
            P("seq", None),
            P("seq", None),
            P("seq", None),
            P("seq", None),
            P("seq"),
            P("seq"),
            P("seq"),
            P("seq", None),
        ),
        check_vma=False,
    )
```

profile of v0, /device:TPU:0, one launch (start us, length us, event | category | flops | bytes accessed | tf_op | source)
XLA Modules:
  0.0 1007.6 jit_solution(6008069518649326751)
XLA Ops:
  9.3 2.7 convolution_convert_fusion.23
  12.0 2.8 convolution_convert_fusion.25
  14.9 2.5 convolution_convert_fusion.20
  23.0 5.9 fusion.3
  28.9 5.9 fusion.1
  37.2 9.5 copy.118
  46.7 9.2 copy.121
  63.4 14.8 %all-gather.11.cloned.1.call-done = bf16[1024,768]{1,0:T(8,128)(2,1)} async-done(((bf16[256,768]{1,0:T(8,128)(2,1)}), bf16[1024,768]{1,0:T(8,128)(2,1)}) %all-gather.11.cloned.1.call-update) | async-done | bytes 1572880 | tf_op jit(solution)/shard_map/all_gather | solution.py:217
  82.9 17.0 %all-gather.9.cloned.1.call-done = bf16[1024,768]{1,0:T(8,128)(2,1)} async-done(((bf16[256,768]{1,0:T(8,128)(2,1)}), bf16[1024,768]{1,0:T(8,128)(2,1)}) %all-gather.9.cloned.1.call-update) | async-done | bytes 1572880 | tf_op jit(solution)/shard_map/all_gather | solution.py:218
  99.8 2.6 fusion.122
  111.9 4.6 fusion.128
  123.9 2.8 fusion.130
  132.3 3.5 exponential_reduce_fusion
  137.5 2.7 fusion.131
  140.9 9.3 multiply_convert_fusion.4
  158.8 4.4 convolution_convert_fusion.10
  168.0 4.5 multiply_convert_fusion.2
  180.5 3.1 fusion.132
  187.8 4.1 convolution_convert_fusion.14
  191.9 4.0 convolution_convert_fusion.15
  198.8 4.3 multiply_convert_fusion
  210.5 2.7 convolution_convert_fusion.2
  213.3 2.8 convolution_convert_fusion.5
  217.8 3.4 fusion.133
  224.8 2.5 fusion.21
  235.2 21.1 %reduce-scatter.21.cloned.1.call-done = bf16[256,768]{0,1:T(8,128)(2,1)} async-done(((bf16[1024,768]{0,1:T(8,128)(2,1)}), bf16[256,768]{0,1:T(8,128)(2,1)}) %reduce-scatter.21.cloned.1.call-update) | async-done | bytes 393232 | tf_op jit(solution)/shard_map/reduce_scatter | solution.py:293
  256.3 2.7 convolution_convert_fusion.7
  259.0 28.7 %reduce-scatter.19.cloned.1.call-done = bf16[256,768]{0,1:T(8,128)(2,1)} async-done(((bf16[1024,768]{0,1:T(8,128)(2,1)}), bf16[256,768]{0,1:T(8,128)(2,1)}) %reduce-scatter.19.cloned.1.call-update) | async-done | bytes 393232 | tf_op jit(solution)/shard_map/reduce_scatter | solution.py:290
  287.7 2.6 convolution_convert_fusion.8
  290.5 5.1 convolution_convert_fusion.1
  296.6 5.2 convolution_convert_fusion
  304.3 7.9 copy.130
  312.2 7.9 copy.131
  320.0 2.7 fusion.134
  322.7 5.0 fusion.29
  327.7 3.2 fusion.32
  333.1 11.3 %reduce-scatter.35.cloned.1.call-done = bf16[192,768]{1,0:T(8,128)(2,1)} async-done(((bf16[768,768]{1,0:T(8,128)(2,1)}), bf16[192,768]{1,0:T(8,128)(2,1)}) %reduce-scatter.35.cloned.1.call-update) | async-done | bytes 294928 | tf_op jit(solution)/shard_map/reduce_scatter | solution.py:325
  344.4 28.3 %reduce-scatter.33.cloned.1.call-done = bf16[192,768]{1,0:T(8,128)(2,1)} async-done(((bf16[768,768]{1,0:T(8,128)(2,1)}), bf16[192,768]{1,0:T(8,128)(2,1)}) %reduce-scatter.33.cloned.1.call-update) | async-done | bytes 294928 | tf_op jit(solution)/shard_map/reduce_scatter | solution.py:322
  372.7 28.3 %reduce-scatter.27.cloned.1.call-done = bf16[192,768]{1,0:T(8,128)(2,1)} async-done(((bf16[768,768]{1,0:T(8,128)(2,1)}), bf16[192,768]{1,0:T(8,128)(2,1)}) %reduce-scatter.27.cloned.1.call-update) | async-done | bytes 294928 | tf_op jit(solution)/shard_map/reduce_scatter | solution.py:313
  404.5 10.9 %all-reduce.5 = (bf16[768]{0:T(1024)(128)(2,1)S(1)}, bf16[768]{0:T(1024)(128)(2,1)S(1)}, bf16[768]{0:T(1024)(128)(2,1)S(1)}, bf16[32,12]{1,0:T(8,128)(2,1)S(1)}) all-reduce(bf16[768]{0:T(1024)(128)(2,1)S(1)} %get-tuple-element.89, bf16[768]{0:T(1024)(128)(2,1)} %get-tuple-element.87, ...), channel_id=16, replica_groups=mesh['dp'=8,'seq'=4] {'seq'}, use_global_device_ids=true, to_apply=%region_45.46.clone | all-reduce | flops 2688 | bytes 10752
  420.0 2.8 fusion.22
  423.9 5.5 reduce-scatter.45.cloned.1.call-done
  430.5 27.2 %reduce-scatter.43.cloned.1.call-done = bf16[192,768]{1,0:T(8,128)(2,1)} async-done(((bf16[768,768]{1,0:T(8,128)(2,1)}), bf16[192,768]{1,0:T(8,128)(2,1)}) %reduce-scatter.43.cloned.1.call-update) | async-done | bytes 294928
  458.9 27.0 %reduce-scatter.31.cloned.1.call-done = bf16[192,768]{1,0:T(8,128)(2,1)} async-done(((bf16[768,768]{1,0:T(8,128)(2,1)}), bf16[192,768]{1,0:T(8,128)(2,1)}) %reduce-scatter.31.cloned.1.call-update) | async-done | bytes 294928 | tf_op jit(solution)/shard_map/reduce_scatter | solution.py:319
  485.9 28.9 %reduce-scatter.29.cloned.1.call-done = bf16[192,768]{1,0:T(8,128)(2,1)} async-done(((bf16[768,768]{1,0:T(8,128)(2,1)}), bf16[192,768]{1,0:T(8,128)(2,1)}) %reduce-scatter.29.cloned.1.call-update) | async-done | bytes 294928 | tf_op jit(solution)/shard_map/reduce_scatter | solution.py:316
  514.8 50.3 %reduce-scatter.39.cloned.1.call-done = bf16[192,3072]{1,0:T(8,128)(2,1)} async-done(((bf16[768,3072]{1,0:T(8,128)(2,1)}), bf16[192,3072]{1,0:T(8,128)(2,1)}) %reduce-scatter.39.cloned.1.call-update) | async-done | bytes 1179664 | tf_op jit(solution)/shard_map/reduce_scatter | solution.py:337
  565.1 50.5 %reduce-scatter.41.cloned.1.call-done = bf16[768,768]{1,0:T(8,128)(2,1)} async-done(((bf16[3072,768]{1,0:T(8,128)(2,1)}), bf16[768,768]{1,0:T(8,128)(2,1)}) %reduce-scatter.41.cloned.1.call-update) | async-done | bytes 1179664 | tf_op jit(solution)/shard_map/reduce_scatter | solution.py:340
  615.5 382.9 %all-reduce.7 = (f32[192,768]{1,0:T(8,128)}, f32[192,768]{1,0:T(8,128)}, f32[192,768]{1,0:T(8,128)}, f32[192,768]{1,0:T(8,128)}, f32[192,768]{1,0:T(8,128)}, /*i...) all-reduce(bf16[192,768]{1,0:T(8,128)(2,1)} %reduce-scatter.27.clon, ...), channel_id=1, replica_groups=mesh['dp'=8,'seq'=4] {'dp'}, use_global_device_ids=true, to_apply=%region_25.26 | all-reduce | flops 2359968 | bytes 14161152 | tf_op jit(solution)/shard_map/psum | solution.py:311
  (368 shorter events, 113.0 us)
Async XLA Ops:
  7.2 120.2 %copy-start = (bf16[768,768]{1,0:T(8,128)(2,1)S(1)}, bf16[768,768]{1,0:T(8,128)(2,1)}, u32[]{:S(2)}) copy-start(bf16[768,768]{1,0:T(8,128)(2,1)} %param.28) | copy-start | bytes 3538948
  7.2 7.7 copy-start.39
  7.2 50.0 %all-gather.7.cloned.1.call-start = ((), (), s32[]{:S(2)}) async-start(), calls=%async_computation.15 | async-start | bytes 1966080 | tf_op jit(solution)/shard_map/all_gather | solution.py:204
  8.6 10.4 %copy-start.77 = (f32[256]{0:T(256)}, f32[256]{0:T(256)S(1)}, u32[]{:S(2)}) copy-start(f32[256]{0:T(256)S(1)} %fusion.108) | copy-start | bytes 3076
  9.3 9.7 copy-start.70
  12.0 6.8 copy-start.92
  12.0 7.0 copy-start.11
  12.0 48.8 %all-gather.5.cloned.1.call-start = ((), (), s32[]{:S(2)}) async-start(), calls=%async_computation.14 | async-start | bytes 1966080 | tf_op jit(solution)/shard_map/all_gather | solution.py:205
  14.8 63.3 %all-gather.11.cloned.1.call-start = ((), (), s32[]{:S(2)}) async-start(), calls=%async_computation.17 | async-start | bytes 1966080 | tf_op jit(solution)/shard_map/all_gather | solution.py:217
  17.4 82.4 %all-gather.9.cloned.1.call-start = ((), (), s32[]{:S(2)}) async-start(), calls=%async_computation.16 | async-start | bytes 1966080 | tf_op jit(solution)/shard_map/all_gather | solution.py:218
  18.7 206.1 %reduce-scatter.25.cloned.1.call-start = ((), (), s32[]{:S(2)}) async-start(), calls=%async_computation.21 | async-start | bytes 1966080 | tf_op jit(solution)/shard_map/reduce_scatter | solution.py:258
  22.8 6.1 copy-start.58
  28.9 6.2 copy-start.90
  28.9 6.8 copy-start.91
  109.4 8.6 slice-start.6
  111.9 6.1 slice-start.7
  127.3 13.0 %copy-start.8 = (f32[256,768]{1,0:T(8,128)}, f32[256,768]{1,0:T(8,128)S(1)}, u32[]{:S(2)}) copy-start(f32[256,768]{1,0:T(8,128)S(1)} %get-tuple-element.136) | copy-start | bytes 2359300
  131.1 6.4 copy-start.3
  140.2 10.0 copy-start.50
  140.2 10.0 slice-start.10
  140.9 13.6 %copy-start.28 = (f32[256,768]{1,0:T(8,128)}, f32[256,768]{1,0:T(8,128)S(1)}, u32[]{:S(2)}) copy-start(f32[256,768]{1,0:T(8,128)S(1)} %get-tuple-element.144) | copy-start | bytes 2359300
  140.9 13.6 %copy-start.83 = (f32[256]{0:T(256)}, f32[256]{0:T(256)S(1)}, u32[]{:S(2)}) copy-start(f32[256]{0:T(256)S(1)} %fusion.110) | copy-start | bytes 3076
  140.9 9.3 copy-start.61
  140.9 9.3 slice-start.11
  154.5 8.8 slice-start.2
  166.4 6.8 slice-start.4
  166.4 63.3 %reduce-scatter.23.cloned.1.call-start = ((), (), s32[]{:S(2)}) async-start(), calls=%async_computation.20 | async-start | bytes 1966080 | tf_op jit(solution)/shard_map/reduce_scatter | solution.py:255
  180.2 76.1 %reduce-scatter.21.cloned.1.call-start = ((), (), s32[]{:S(2)}) async-start(), calls=%async_computation.19 | async-start | bytes 1966080 | tf_op jit(solution)/shard_map/reduce_scatter | solution.py:293
  195.9 7.9 slice-start
  197.4 90.4 %reduce-scatter.19.cloned.1.call-start = ((), (), s32[]{:S(2)}) async-start(), calls=%async_computation.18 | async-start | bytes 1966080 | tf_op jit(solution)/shard_map/reduce_scatter | solution.py:290
  210.5 122.6 %reduce-scatter.37.cloned.1.call-start = ((), (), s32[]{:S(2)}) async-start(), calls=%async_computation.27 | async-start | bytes 1474560 | tf_op jit(solution)/shard_map/reduce_scatter | solution.py:334
  213.2 131.2 %reduce-scatter.35.cloned.1.call-start = ((), (), s32[]{:S(2)}) async-start(), calls=%async_computation.26 | async-start | bytes 1474560 | tf_op jit(solution)/shard_map/reduce_scatter | solution.py:325
  216.1 156.6 %reduce-scatter.33.cloned.1.call-start = ((), (), s32[]{:S(2)}) async-start(), calls=%async_computation.25 | async-start | bytes 1474560 | tf_op jit(solution)/shard_map/reduce_scatter | solution.py:322
  217.7 183.4 %reduce-scatter.27.cloned.1.call-start = ((), (), s32[]{:S(2)}) async-start(), calls=%async_computation.22 | async-start | bytes 1474560 | tf_op jit(solution)/shard_map/reduce_scatter | solution.py:313
  224.7 204.7 %reduce-scatter.45.cloned.1.call-start = ((), (), s32[]{:S(2)}) async-start(), calls=%async_computation.31 | async-start | bytes 1474560
  229.7 228.0 %reduce-scatter.43.cloned.1.call-start = ((), (), s32[]{:S(2)}) async-start(), calls=%async_computation.30 | async-start | bytes 1474560
  234.7 55.8 %copy-start.29 = (f32[256,768]{1,0:T(8,128)S(1)}, f32[256,768]{1,0:T(8,128)}, u32[]{:S(2)}) copy-start(f32[256,768]{1,0:T(8,128)} %copy-done.28) | copy-start | bytes 2359300
  234.7 55.8 %copy-start.73 = (f32[768]{0:T(1024)S(1)}, f32[768]{0:T(1024)}, u32[]{:S(2)}) copy-start(f32[768]{0:T(1024)} %convert_element_type.609) | copy-start | bytes 9220
  234.7 55.8 %copy-start.84 = (f32[256]{0:T(256)S(1)}, f32[256]{0:T(256)}, u32[]{:S(2)}) copy-start(f32[256]{0:T(256)} %copy-done.83) | copy-start | bytes 3076
  234.7 251.2 %reduce-scatter.31.cloned.1.call-start = ((), (), s32[]{:S(2)}) async-start(), calls=%async_computation.24 | async-start | bytes 1474560 | tf_op jit(solution)/shard_map/reduce_scatter | solution.py:319
  259.0 255.8 %reduce-scatter.29.cloned.1.call-start = ((), (), s32[]{:S(2)}) async-start(), calls=%async_computation.23 | async-start | bytes 1474560 | tf_op jit(solution)/shard_map/reduce_scatter | solution.py:316
  290.4 274.7 %reduce-scatter.39.cloned.1.call-start = ((), (), s32[]{:S(2)}) async-start(), calls=%async_computation.28 | async-start | bytes 5898240 | tf_op jit(solution)/shard_map/reduce_scatter | solution.py:337
  295.6 319.9 %reduce-scatter.41.cloned.1.call-start = ((), (), s32[]{:S(2)}) async-start(), calls=%async_computation.29 | async-start | bytes 5898240 | tf_op jit(solution)/shard_map/reduce_scatter | solution.py:340
  312.2 7.9 copy-start.52
  322.7 8.2 slice-start.12
  333.1 70.2 %copy-start.64 = (bf16[256,768]{0,1:T(8,128)(2,1)S(1)}, bf16[256,768]{0,1:T(8,128)(2,1)}, u32[]{:S(2)}) copy-start(bf16[256,768]{0,1:T(8,128)(2,1)} %reduce-scatter.21.cloned.1.call-done) | copy-start | bytes 1179652
  333.1 84.3 %copy-start.88 = (f32[256]{0:T(256)S(1)}, f32[256]{0:T(256)}, u32[]{:S(2)}) copy-start(f32[256]{0:T(256)} %copy-done.87) | copy-start | bytes 3076
  420.0 195.5 %copy-start.89 = (f32[192]{0:T(256)S(1)}, f32[192]{0:T(256)}, u32[]{:S(2)}) copy-start(f32[192]{0:T(256)} %dynamic-slice_convert_fusion.3) | copy-start | bytes 2308
  (79 other events, 220.9 us)
Sparse Core Ops, SparseCore 0:
  12.1 22.4 all-gather.6
  36.7 19.5 all-gather.4
  58.4 19.6 all-gather.10
  80.1 19.6 all-gather.8
  166.6 28.1 reduce-scatter.24
  197.3 28.1 reduce-scatter.22
  228.1 28.1 reduce-scatter.20
  259.5 28.1 reduce-scatter.18
  290.3 25.7 reduce-scatter.36
  318.7 25.7 reduce-scatter.34
  347.0 25.7 reduce-scatter.32
  375.3 25.7 reduce-scatter.26
  403.6 25.7 reduce-scatter.44
  432.0 25.7 reduce-scatter.42
  460.1 25.7 reduce-scatter.30
  489.0 25.6 reduce-scatter.28
  517.2 47.8 reduce-scatter.38
  567.6 47.8 reduce-scatter.40
where the time goes:
time: 1020 us; the launch traced here: 1010 us
  blocking collectives  394 us (39%)
  waiting for transfers between devices  339 us (33%)
  matrix products  148 us (15%)
  local copies, waits for them, and re-layouts  82.4 us (8%)
  other arithmetic  25.6 us (3%)
  between operations  17.4 us (2%)
    psum x1, blocking collectives, on_device(): lax.psum((lax.psum_scatter(grad_self_query.astype(jnp.bfloat16), 'seq', s...  383 us
    reduce_scatter x1, waiting for transfers between devices, on_device(): lax.psum_scatter(grad_ffn_out.astype(jnp.bfloat16), 'seq', scatter_dimens...  50.5 us
    reduce_scatter x1, waiting for transfers between devices, on_device(): lax.psum_scatter(grad_ffn_in.astype(jnp.bfloat16), 'seq', scatter_dimensi...  50.3 us
    unnamed x20, waiting for transfers between devices  33 us
    dot_general x10, matrix products, matmul_left_t(): lax.dot_general(left, right, (((0,), (0,)), ((), ())), preferred_element_...  29.2 us
    reduce_scatter x1, waiting for transfers between devices, on_device(): lax.psum_scatter(grad_self_key.astype(jnp.bfloat16), 'seq', scatter_dimen...  28.9 us
    reduce_scatter x1, waiting for transfers between devices, on_device(): lax.psum_scatter(key_part.astype(jnp.bfloat16), 'seq', scatter_dimension=...  28.7 us
    reduce_scatter x1, waiting for transfers between devices, on_device(): lax.psum_scatter(grad_self_query.astype(jnp.bfloat16), 'seq', scatter_dim...  28.3 us
  transfers between devices with their start and end apart: 18, of which 13 were waited for; matrix products, arithmetic and copies ran while one was open for 17% of the time, Pallas kernels for 0%

commit v1 on v0

--- a/solution.py
+++ b/solution.py
@@ -1,8 +1,11 @@
+import functools
 import math
 
 import jax
 import jax.numpy as jnp
 from jax import lax
+from jax.experimental import pallas as pl
+from jax.experimental.pallas import tpu as pltpu
 from jax.sharding import PartitionSpec as P
 
 EPS = 1e-06
@@ -146,6 +149,266 @@
         jnp.concatenate(value_parts, axis=0),
         table_grad,
     )
+
+
+MESH = pl.DeviceIdType.MESH
+
+
+def add_low(left, right):
+    return (left.astype(jnp.float32) + right.astype(jnp.float32)).astype(jnp.bfloat16)
+
+
+def reduce_kernel(
+    planes,
+    piece,
+    chunks,
+    big_hbm,
+    small_in,
+    fin,
+    small_out,
+    kept,
+    core_recv,
+    y_recv,
+    x_recv,
+    z_recv,
+    small_a,
+    small_c,
+    small_y,
+    small_x,
+    small_z,
+    load_sem,
+    core_sem,
+    y_sem,
+    x_sem,
+    z_sem,
+    gz_sem,
+    gx_sem,
+    tiny_sem,
+):
+    row = lax.axis_index("dp")
+    place = lax.axis_index("seq")
+    side, core = place // 2, lax.rem(place, 2)
+    plane, half = row // 2, lax.rem(row, 2)
+    core_peer = (row, side * 2 + 1 - core)
+    y_peer = (row, (1 - side) * 2 + core)
+    x_peer = (plane * 2 + 1 - half, place)
+
+    def z_peer(step):
+        return (lax.rem(plane + step, planes) * 2 + half, place)
+
+    half_rows = piece * planes
+    chunk_rows = 2 * half_rows
+
+    def span(first, size):
+        return pl.ds(pl.multiple_of(first, piece), size)
+
+    def chunk_span(index):
+        return span(index * chunk_rows, chunk_rows)
+
+    def send(src, dst, sems, slot, peer):
+        return pltpu.make_async_remote_copy(
+            src_ref=src,
+            dst_ref=dst,
+            send_sem=sems.at[(0, *slot)],
+            recv_sem=sems.at[(1, *slot)],
+            device_id=peer,
+            device_id_type=MESH,
+        )
+
+    def load(index):
+        rows = chunk_span(index)
+        return pltpu.make_async_copy(
+            big_hbm.at[core, :, rows], kept.at[:, rows], load_sem.at[index]
+        )
+
+    def core_copy(index):
+        rows = chunk_span(index)
+        return send(
+            big_hbm.at[1 - core, :, rows], core_recv.at[:, rows], core_sem, (index,), core_peer
+        )
+
+    def y_copy(index):
+        rows = chunk_span(index)
+        return send(kept.at[1 - side, rows], y_recv.at[rows], y_sem, (index,), y_peer)
+
+    def x_copy(index):
+        other = span(index * chunk_rows + (1 - half) * half_rows, half_rows)
+        return send(
+            kept.at[side, other], x_recv.at[span(index * half_rows, half_rows)], x_sem, (index,), x_peer
+        )
+
+    def z_rows(index, which):
+        return span(index * chunk_rows + half * half_rows + which * piece, piece)
+
+    def z_copy(index, step):
+        target = lax.rem(plane + step, planes)
+        return send(
+            kept.at[side, z_rows(index, target)],
+            z_recv.at[step - 1, span(index * piece, piece)],
+            z_sem,
+            (index, step - 1),
+            z_peer(step),
+        )
+
+    def gz_copy(index, step):
+        rows = z_rows(index, plane)
+        return send(fin.at[rows], fin.at[rows], gz_sem, (index, step - 1), z_peer(step))
+
+    def gx_copy(index):
+        rows = span(index * chunk_rows + half * half_rows, half_rows)
+        return send(fin.at[rows], fin.at[rows], gx_sem, (index,), x_peer)
+
+    barrier = pltpu.get_barrier_semaphore()
+    peers = [core_peer, y_peer, x_peer] + [z_peer(step) for step in range(1, planes)]
+    for peer in peers:
+        pl.semaphore_signal(barrier, inc=1, device_id=peer, device_id_type=MESH)
+    pl.semaphore_wait(barrier, len(peers))
+
+    tiny_core = send(small_in.at[1 - core], small_c, tiny_sem, (0,), core_peer)
+    tiny_core.start()
+
+    def begin(index, carry):
+        load(index).start()
+        core_copy(index).start()
+        return carry
+
+    lax.fori_loop(0, chunks, begin, 0)
+
+    tiny_core.wait()
+    small_a[...] = small_in[core] + small_c[...]
+    tiny_y = send(small_a.at[1 - side], small_y, tiny_sem, (1,), y_peer)
+    tiny_y.start()
+
+    def tick(step, carry):
+        @pl.when(step < chunks)
+        def _():
+            load(step).wait()
+            core_copy(step).wait()
+            rows = chunk_span(step)
+            for other in range(2):
+                kept[other, rows, :] = add_low(kept[other, rows, :], core_recv[other, rows, :])
+            y_copy(step).start()
+
+        @pl.when((step >= 2) & (step < chunks + 2))
+        def _():
+            index = step - 2
+            y_copy(index).wait()
+            rows = chunk_span(index)
+            kept[side, rows, :] = add_low(kept[side, rows, :], y_recv[rows, :])
+            x_copy(index).start()
+
+        @pl.when((step >= 4) & (step < chunks + 4))
+        def _():
+            index = step - 4
+            x_copy(index).wait()
+            rows = span(index * chunk_rows + half * half_rows, half_rows)
+            kept[side, rows, :] = add_low(
+                kept[side, rows, :], x_recv[span(index * half_rows, half_rows), :]
+            )
+            for step_z in range(1, planes):
+                z_copy(index, step_z).start()
+
+        @pl.when((step >= 6) & (step < chunks + 6))
+        def _():
+            index = step - 6
+            total = kept[side, z_rows(index, plane), :].astype(jnp.float32)
+            for step_z in range(1, planes):
+                z_copy(index, step_z).wait()
+                total = total + z_recv[step_z - 1, span(index * piece, piece), :].astype(jnp.float32)
+            fin[z_rows(index, plane), :] = total.astype(jnp.bfloat16)
+            for step_z in range(1, planes):
+                gz_copy(index, step_z).start()
+
+        @pl.when((step >= 8) & (step < chunks + 8))
+        def _():
+            index = step - 8
+            for step_z in range(1, planes):
+                gz_copy(index, step_z).wait()
+            gx_copy(index).start()
+
+        @pl.when(step >= 10)
+        def _():
+            gx_copy(step - 10).wait()
+
+        return carry
+
+    lax.fori_loop(0, chunks + 10, tick, 0)
+
+    tiny_y.wait()
+    small_out[...] = small_a[side] + small_y[...]
+    tiny_x = send(small_out, small_x, tiny_sem, (2,), x_peer)
+    tiny_x.start()
+    tiny_x.wait()
+    small_y[...] = small_out[...] + small_x[...]
+    copies = []
+    for step in range(1, planes):
+        copy = send(small_y, small_z.at[step - 1], tiny_sem, (2 + step,), z_peer(step))
+        copy.start()
+        copies.append(copy)
+    for copy in copies:
+        copy.wait()
+    total = small_y[...]
+    for step in range(1, planes):
+        total = total + small_z[step - 1]
+    small_out[...] = total
+
+
+def reduce_grads(big, small, rows_all):
+    planes = rows_all // 2
+    count, width = big.shape[2:]
+    piece = 16
+    chunk_rows = 2 * planes * piece
+    chunks = count // chunk_rows
+    tall = small.shape[2]
+    tiny = (tall, width)
+    return pl.pallas_call(
+        functools.partial(reduce_kernel, planes, piece, chunks),
+        out_shape=(
+            jax.ShapeDtypeStruct((count, width), jnp.bfloat16),
+            jax.ShapeDtypeStruct(tiny, jnp.float32),
+        ),
+        in_specs=[
+            pl.BlockSpec(memory_space=pl.ANY),
+            pl.BlockSpec(memory_space=pltpu.VMEM),
+        ],
+        out_specs=[pl.BlockSpec(memory_space=pltpu.VMEM)] * 2,
+        scratch_shapes=[
+            pltpu.VMEM((2, count, width), jnp.bfloat16),
+            pltpu.VMEM((2, count, width), jnp.bfloat16),
+            pltpu.VMEM((count, width), jnp.bfloat16),
+            pltpu.VMEM((count // 2, width), jnp.bfloat16),
+            pltpu.VMEM((planes - 1, chunks * piece, width), jnp.bfloat16),
+            pltpu.VMEM((2, *tiny), jnp.float32),
+            pltpu.VMEM((2, *tiny), jnp.float32),
+            pltpu.VMEM(tiny, jnp.float32),
+            pltpu.VMEM(tiny, jnp.float32),
+            pltpu.VMEM((planes - 1, *tiny), jnp.float32),
+            pltpu.SemaphoreType.DMA((chunks,)),
+            pltpu.SemaphoreType.DMA((2, chunks)),
+            pltpu.SemaphoreType.DMA((2, chunks)),
+            pltpu.SemaphoreType.DMA((2, chunks)),
+            pltpu.SemaphoreType.DMA((2, chunks, planes - 1)),
+            pltpu.SemaphoreType.DMA((2, chunks, planes - 1)),
+            pltpu.SemaphoreType.DMA((2, chunks)),
+            pltpu.SemaphoreType.DMA((2, 2 + planes)),
+        ],
+        compiler_params=pltpu.CompilerParams(
+            collective_id=0, has_side_effects=True, vmem_limit_bytes=56 * 2**20
+        ),
+        name="reduce_grads",
+    )(big, small)
+
+
+def by_place(grad):
+    width = 768
+    parts = grad.shape[0] // 4
+    pieces = grad.reshape(2, 2, parts, grad.shape[1])
+    pieces = jnp.transpose(pieces, (1, 0, 2, 3))
+    if grad.shape[1] == width:
+        return pieces
+    blocks = grad.shape[1] // width
+    pieces = pieces.reshape(2, 2, parts, blocks, width)
+    return jnp.transpose(pieces, (0, 1, 3, 2, 4)).reshape(2, 2, parts * blocks, width)
 
 
 def on_device(
@@ -308,71 +571,61 @@
     _, self_norm_back = jax.vjp(norm_rows, states, gain_one)
     state_part, gain_self_grad = self_norm_back(normed_grad)
     dec_grad = first_grad + state_part
-    summed = lax.psum(
-        (
-            lax.psum_scatter(
-                grad_self_query.astype(jnp.bfloat16), "seq", scatter_dimension=0, tiled=True
-            ).astype(jnp.float32),
-            lax.psum_scatter(
-                grad_self_key.astype(jnp.bfloat16), "seq", scatter_dimension=0, tiled=True
-            ).astype(jnp.float32),
-            lax.psum_scatter(
-                grad_self_value.astype(jnp.bfloat16), "seq", scatter_dimension=0, tiled=True
-            ).astype(jnp.float32),
-            lax.psum_scatter(
-                grad_self_output.astype(jnp.bfloat16), "seq", scatter_dimension=0, tiled=True
-            ).astype(jnp.float32),
-            lax.psum_scatter(
-                grad_cross_query.astype(jnp.bfloat16), "seq", scatter_dimension=0, tiled=True
-            ).astype(jnp.float32),
-            lax.psum_scatter(
-                grad_cross_key.astype(jnp.bfloat16), "seq", scatter_dimension=0, tiled=True
-            ).astype(jnp.float32),
-            lax.psum_scatter(
-                grad_cross_value.astype(jnp.bfloat16), "seq", scatter_dimension=0, tiled=True
-            ).astype(jnp.float32),
-            lax.psum_scatter(
-                grad_cross_output.astype(jnp.bfloat16), "seq", scatter_dimension=0, tiled=True
-            ).astype(jnp.float32),
-            lax.psum_scatter(
-                grad_ffn_in.astype(jnp.bfloat16), "seq", scatter_dimension=0, tiled=True
-            ).astype(jnp.float32),
-            lax.psum_scatter(
-                grad_ffn_out.astype(jnp.bfloat16), "seq", scatter_dimension=0, tiled=True
-            ).astype(jnp.float32),
-            lax.psum_scatter(
-                gain_self_grad.astype(jnp.bfloat16), "seq", scatter_dimension=0, tiled=True
-            ).astype(jnp.float32),
-            lax.psum_scatter(
-                gain_cross_grad.astype(jnp.bfloat16), "seq", scatter_dimension=0, tiled=True
-            ).astype(jnp.float32),
-            lax.psum_scatter(
-                gain_ffn_grad.astype(jnp.bfloat16), "seq", scatter_dimension=0, tiled=True
-            ).astype(jnp.float32),
-            lax.psum_scatter(
-                bias_grad.astype(jnp.bfloat16), "seq", scatter_dimension=0, tiled=True
-            ).astype(jnp.float32),
-        ),
-        "dp",
-    )
+    width = dec_states.shape[2]
+    fan = ffn_in.shape[1] // width
+    own = width // 4
+    big = jnp.concatenate(
+        [
+            by_place(grad.astype(jnp.bfloat16))
+            for grad in (
+                grad_ffn_out,
+                grad_ffn_in,
+                grad_cross_output,
+                grad_cross_query,
+                grad_cross_key,
+                grad_cross_value,
+                grad_self_output,
+                grad_self_query,
+                grad_self_key,
+                grad_self_value,
+            )
+        ],
+        axis=2,
+    )
+    gains = jnp.stack([gain_self_grad, gain_cross_grad, gain_ffn_grad]).reshape(3, 4, own)
+    gains = jnp.transpose(gains, (1, 0, 2))
+    gains = jnp.pad(gains, ((0, 0), (0, 0), (0, width - own)))
+    near = bias_grad.reshape(4, 1, -1)
+    near = jnp.pad(near, ((0, 0), (0, 4), (0, width - near.shape[2])))
+    small = jnp.concatenate([gains, near], axis=1)
+    small = jnp.transpose(small.reshape(2, 2, 8, width), (1, 0, 2, 3))
+    summed, tiny = reduce_grads(big, small, lax.axis_size("dp"))
+
+    def rows(first, count):
+        return summed[first : first + count].astype(jnp.float32)
+
+    tall = own * fan
+    out_ffn_in = jnp.transpose(rows(tall, tall).reshape(fan, own, width), (1, 0, 2))
+    base = 2 * tall
+    heads_own = bias_grad.shape[0] // 4
     return (
         layer_out[None],
         dec_grad[None],
         enc_grad[None],
-        summed[0],
-        summed[1],
-        summed[2],
-        summed[3],
-        summed[4],
-        summed[5],
-        summed[6],
-        summed[7],
-        summed[8],
-        summed[9],
-        summed[10],
-        summed[11],
-        summed[12],
-        summed[13],
+        rows(base + 5 * own, own),
+        rows(base + 6 * own, own),
+        rows(base + 7 * own, own),
+        rows(base + 4 * own, own),
+        rows(base + own, own),
+        rows(base + 2 * own, own),
+        rows(base + 3 * own, own),
+        rows(base, own),
+        out_ffn_in.reshape(own, fan * width),
+        rows(0, tall),
+        tiny[0, :own],
+        tiny[1, :own],
+        tiny[2, :own],
+        tiny[3, : heads_own * heads].reshape(heads_own, heads),
     )
 
 

time: 1020 us -> 490 us (0.48)
  blocking collectives: 394 us -> 0 us
  waiting for transfers between devices: 339 us -> 32 us
  Pallas kernels: 0 us -> 146 us
  local copies, waits for them, and re-layouts: 82.4 us -> 116 us
    psum x1 -> x0, blocking collectives: 383 us -> none  [on_device(): lax.psum((lax.psum_scatter(grad_self_query.astype(jnp.bfloat16), 'seq', s...]
    reduce_scatter x8 -> x0, waiting for transfers between devices: 225 us -> none  [the longest x1 50.5 us: on_device(): lax.psum_scatter(grad_ffn_out.astype(jnp.bfloat16), 'seq', scatter_dimens...]
    pallas_call x0 -> x1, Pallas kernels: none -> 146 us  [reduce_grads(): pl.pallas_call(functools.partial(reduce_kernel, planes, piece, chunks), o...]
    unnamed x20 -> x8, waiting for transfers between devices: 33 us -> 0.13 us
    reduce_scatter x1, waiting for transfers between devices: 28.7 us -> 0.01 us  [on_device(): lax.psum_scatter(key_part.astype(jnp.bfloat16), 'seq', scatter_dimension=...]
    reduce_scatter x1, waiting for transfers between devices: 21.1 us -> 0.01 us  [on_device(): lax.psum_scatter(value_part.astype(jnp.bfloat16), 'seq', scatter_dimensio...]
    reshape x0 -> x5, local copies, waits for them, and re-layouts: none -> 18.6 us  [the longest x1 9.96 us: by_place(): pieces = pieces.reshape(2, 2, parts, blocks, width)]
    dot_general x10, matrix products: 29.2 us -> 15.1 us  [matmul_left_t(): lax.dot_general(left, right, (((0,), (0,)), ((), ())), preferred_element_...]
  transfers between devices with their start and end apart: 18 -> 8, of which waited for: 13 -> 2; matrix products, arithmetic and copies ran while one was open for 17% -> 36% of each run, Pallas kernels for 0% -> 0%
where the time goes in v1:
time: 490 us; the launch traced here: 480 us
  Pallas kernels  146 us (30%)
  matrix products  140 us (29%)
  local copies, waits for them, and re-layouts  116 us (24%)
  waiting for transfers between devices  32 us (7%)
  other arithmetic  29.8 us (6%)
  between operations  16.2 us (3%)
    pallas_call x1, Pallas kernels, reduce_grads(): pl.pallas_call(functools.partial(reduce_kernel, planes, piece, chunks), o...  146 us
    dot_general x10, matrix products, matmul(): return jnp.dot(left, right, preferred_element_type=jnp.float32)  27.8 us
    unnamed x249, local copies, waits for them, and re-layouts  21.2 us
    dot_general x2, local copies, waits for them, and re-layouts, block_scores(): jnp.einsum('skb,bh->hsk', position_terms(start, span), table, preferred_e...  18.7 us
    all_gather x1, waiting for transfers between devices, on_device(): lax.all_gather(cross_values_own, 'seq', axis=0, tiled=True)  17 us
    dot_general x10, matrix products, matmul_right_t(): lax.dot_general(left, right, (((1,), (1,)), ((), ())), preferred_element_...  17 us
    dot_general x4, matrix products, attention_backward(): jnp.einsum('hsk,shd->khd', probs.astype(jnp.bfloat16), grad_heads, prefer...  15.9 us
    convert_element_type x2, local copies, waits for them, and re-layouts, attention_backward(): (probs * (prob_grad - row_terms[:, :, None])).astype(jnp.bfloat16)  15.8 us
  transfers between devices with their start and end apart: 8, of which 2 were waited for; matrix products, arithmetic and copies ran while one was open for 36% of the time, Pallas kernels for 0%

profile of v1, /device:TPU:0, one launch (start us, length us, event | category | flops | bytes accessed | tf_op | source)
XLA Modules:
  0.0 480.4 jit_solution(17974387973361791999)
XLA Ops:
  9.3 2.7 convolution_convert_fusion.23
  12.0 2.8 convolution_convert_fusion.25
  14.9 2.5 convolution_convert_fusion.20
  23.0 5.9 %fusion.3 = f32[256,512,12]{0,2,1:T(8,128)} fusion(s32[256,512]{0,1:T(8,128)S(1)} %copy.110, bf16[32,12]{0,1:T(8,128)(2,1)S(1)} %copy-done.95), kind=kOutput, calls=%fused_computation.5 | convolution fusion | flops 104857600 | bytes 6816512 | tf_op jit(solution)/shard_map/skb,bh->hsk/dot_general | solution.py:53
  28.9 5.9 %fusion.1 = f32[256,512,12]{0,2,1:T(8,128)} fusion(s32[256,512]{0,1:T(8,128)S(1)} %copy.113, bf16[32,12]{0,1:T(8,128)(2,1)S(1)} %copy-done.95), kind=kOutput, calls=%fused_computation.2 | convolution fusion | flops 104857600 | bytes 6816512 | tf_op jit(solution)/shard_map/skb,bh->hsk/dot_general | solution.py:53
  37.2 9.4 %copy.111 = f32[256,512,12]{1,0,2:T(8,128)} copy(f32[256,512,12]{0,2,1:T(8,128)} %fusion.3) | data formatting | bytes 12582912 | tf_op jit(solution)/shard_map/skb,bh->hsk/dot_general | solution.py:53
  46.6 9.2 %copy.114 = f32[256,512,12]{1,0,2:T(8,128)} copy(f32[256,512,12]{0,2,1:T(8,128)} %fusion.1) | data formatting | bytes 12582912 | tf_op jit(solution)/shard_map/skb,bh->hsk/dot_general | solution.py:53
  57.2 2.4 fusion.122
  63.4 14.8 %all-gather.11.cloned.1.call-done = bf16[1024,768]{1,0:T(8,128)(2,1)} async-done(((bf16[256,768]{1,0:T(8,128)(2,1)}), bf16[1024,768]{1,0:T(8,128)(2,1)}) %all-gather.11.cloned.1.call-update) | async-done | bytes 1572880 | tf_op jit(solution)/shard_map/all_gather | solution.py:480
  78.1 2.4 fusion.120
  80.5 2.3 copy.119
  82.8 17.0 %all-gather.9.cloned.1.call-done = bf16[1024,768]{1,0:T(8,128)(2,1)} async-done(((bf16[256,768]{1,0:T(8,128)(2,1)}), bf16[1024,768]{1,0:T(8,128)(2,1)}) %all-gather.9.cloned.1.call-update) | async-done | bytes 1572880 | tf_op jit(solution)/shard_map/all_gather | solution.py:481
  99.8 2.6 fusion.119
  102.4 2.3 copy.120
  104.8 2.3 copy.116
  109.4 2.5 copy.109
  111.8 4.6 fusion.126
  123.8 2.5 fusion.128
  132.0 3.5 exponential_reduce_fusion
  137.2 2.7 fusion.129
  140.6 9.5 %multiply_convert_fusion.4 = (bf16[256,3072]{1,0:T(8,128)(2,1)}, f32[256,3072]{1,0:T(8,128)S(1)}, f32[256,3072]{1,0:T(8,128)S(1)}) fusion(bf16[768,3072]{1,0:T(8,128)(2,1)S(1)} %bitcast.353, f32[256,768]{1,0:T(8,128)S(1)} %get-tuple-element.75, f32[768]{0:T(1024)S(1)} %copy-done.85, f32[256]{0:T(256)S(1)} %fusion.107), kind=kOutput, calls=%fused_computation.39 | convolution fusion | flops 1259667456 | bytes 13373440 | tf_op jit(solution)/shard_map/dot_general | solution.py:33
  160.3 4.5 multiply_convert_fusion.2
  165.1 2.3 multiply_convert_fusion.3
  174.6 4.2 multiply_convert_fusion
  184.3 3.9 convolution_convert_fusion.14
  188.2 4.2 convolution_convert_fusion.15
  193.9 2.5 convolution_convert_fusion.12
  196.5 2.7 convolution_convert_fusion.13
  200.6 5.3 %convolution_convert_fusion.10 = bf16[12,64,512]{2,1,0:T(8,128)(2,1)} fusion(bf16[256,12,64]{0,2,1:T(8,128)(2,1)S(1)} %bitcast.311, f32[12,256,512]{2,1,0:T(8,128)} %copy-done.4, f32[12,256]{1,0:T(8,128)S(1)} %copy-done.82, pred[256,512]{1,0:T(8,128)(4,1)S(1)} %get-tuple-element.56), kind=kOutput, calls=%fused_computation.68 | convolution fusion | flops 206438400 | bytes 7614464 | tf_op jit(solution)/shard_map/hsk,shd->khd/dot_general | solution.py:132
  205.9 2.4 convolution_convert_fusion.11
  208.4 5.1 %convolution_convert_fusion = bf16[768,3072]{1,0:T(8,128)(2,1)} fusion(bf16[256,3072]{1,0:T(8,128)(2,1)} %copy-done.73, f32[256,768]{1,0:T(8,128)S(1)} %copy-done.26, f32[768]{0:T(1024)S(1)} %copy-done.86, f32[256]{0:T(256)S(1)} %copy-done.97), kind=kOutput, calls=%fused_computation.32 | convolution fusion | flops 1210908672 | bytes 7081984 | tf_op jit(solution)/shard_map/dot_general | solution.py:43
  213.5 7.9 %copy.134 = bf16[12,256,512]{1,0,2:T(8,128)(2,1)} copy(bf16[12,256,512]{2,1,0:T(8,128)(2,1)} %copy-done.7) | data formatting | bytes 6291456 | tf_op jit(solution)/shard_map/convert_element_type | solution.py:122
  221.4 7.9 %copy.135 = bf16[12,256,512]{1,0,2:T(8,128)(2,1)} copy(bf16[12,256,512]{2,1,0:T(8,128)(2,1)} %copy-done.6) | data formatting | bytes 6291456 | tf_op jit(solution)/shard_map/convert_element_type | solution.py:122
  229.4 4.9 %copy.152 = bf16[2,2,192,3072]{3,2,0,1:T(8,128)(2,1)} copy(bf16[2,2,192,3072]{3,2,1,0:T(8,128)(2,1)} %bitcast.277) | data formatting | bytes 9437184 | tf_op jit(solution)/shard_map/reshape | solution.py:405
  234.3 10.0 %reshape.651 = bf16[2,2,192,4,768]{4,3,2,1,0:T(4,128)(2,1)} reshape(bf16[2,2,192,3072]{3,2,1,0:T(8,128)(2,1)} %bitcast.281) | data formatting | bytes 9437184 | tf_op jit(solution)/shard_map/reshape | solution.py:410
  244.3 5.4 %copy.125 = bf16[2,2,4,192,768]{4,3,2,1,0:T(8,128)(2,1)} copy(bf16[2,2,4,192,768]{4,2,3,1,0:T(4,128)(2,1)} %bitcast.282) | data formatting | bytes 9437184 | tf_op jit(solution)/shard_map/transpose | solution.py:411
  251.0 3.1 fusion.131
  254.2 3.1 fusion.25
  263.5 2.5 fusion.27
  266.0 2.5 bitcast_dynamic-update-slice_fusion
  268.5 5.5 %fusion.29 = f32[32,12]{0,1:T(8,128)} fusion(f32[32,12]{0,1:T(8,128)S(1)} %fusion.27, bf16[12,256,512]{1,0,2:T(8,128)(2,1)} %copy.135, s32[256,512]{0,1:T(8,128)S(1)} %copy-done.68), kind=kOutput, calls=%fused_computation.115 | convolution fusion | flops 104857984 | bytes 3673088 | tf_op jit(solution)/shard_map/hsk,skb->bh/dot_general | solution.py:140
  274.1 4.9 %constant_dynamic-update-slice_fusion = bf16[2,2,3072,768]{3,2,1,0:T(8,128)(2,1)} fusion(bf16[2,2,3072,768]{3,2,1,0:T(8,128)(2,1)} %bitcast_dynamic-update-slice_fusion, bf16[2,2,768,768]{3,2,1,0:T(8,128)(2,1)} %bitcast.280), kind=kLoop, calls=%fused_computation.208 | loop fusion | bytes 9437184
  288.9 4.8 %fusion.26 = bf16[1,256,768]{2,1,0:T(8,128)(2,1)} fusion(f32[256,768]{1,0:T(8,128)S(1)} %copy-done.27, bf16[256,3072]{1,0:T(8,128)(2,1)S(1)} %copy-done.57, bf16[3072,768]{1,0:T(8,128)(2,1)} %param.33), kind=kOutput, calls=%fused_computation.100 | convolution fusion | flops 1208352768 | bytes 7471104 | tf_op jit(solution)/shard_map/dot_general | solution.py:33
  293.8 2.8 convolution_add_fusion.2
  296.6 3.6 fusion.42
  313.6 145.9 %reduce_grads.1 = (bf16[3072,768]{1,0:T(8,128)(2,1)}, f32[8,768]{1,0:T(8,128)}) custom-call(bf16[2,2,3072,768]{3,2,1,0:T(8,128)(2,1)} %bitcast_dynamic-update-slice_fusion.1.big_hbm, f32[2,2,8,768]{3,2,1,0:T(8,128)} %bitcast.343), custom_call_target="tpu_custom_call" | custom-call | tf_op jit(solution)/shard_map/reduce_grads/pallas_call | solution.py:364
  461.9 3.3 slice_convert_fusion
  465.2 2.2 slice_convert_fusion.1
  (376 shorter events, 96.9 us)
Async XLA Ops:
  7.2 119.9 %copy-start = (bf16[768,768]{1,0:T(8,128)(2,1)S(1)}, bf16[768,768]{1,0:T(8,128)(2,1)}, u32[]{:S(2)}) copy-start(bf16[768,768]{1,0:T(8,128)(2,1)} %param.28) | copy-start | bytes 3538948
  7.2 7.7 %copy-start.38 = (bf16[1,256,768]{2,1,0:T(8,128)(2,1)S(1)}, bf16[1,256,768]{2,1,0:T(8,128)(2,1)}, u32[]{:S(2)}) copy-start(bf16[1,256,768]{2,1,0:T(8,128)(2,1)} %param.20) | copy-start | bytes 1179652
  7.2 50.0 %all-gather.7.cloned.1.call-start = ((), (), s32[]{:S(2)}) async-start(), calls=%async_computation.5 | async-start | bytes 1966080 | tf_op jit(solution)/shard_map/all_gather | solution.py:467
  8.6 10.4 %copy-start.90 = (f32[256]{0:T(256)}, f32[256]{0:T(256)S(1)}, u32[]{:S(2)}) copy-start(f32[256]{0:T(256)S(1)} %fusion.105) | copy-start | bytes 3076
  9.3 9.7 %copy-start.83 = (f32[768]{0:T(1024)}, f32[768]{0:T(1024)S(1)}, u32[]{:S(2)}) copy-start(f32[768]{0:T(1024)S(1)} %convert_element_type.537) | copy-start | bytes 9220
  11.9 5.5 %copy-start.44 = (bf16[768,768]{1,0:T(8,128)(2,1)S(1)}, bf16[768,768]{1,0:T(8,128)(2,1)}, u32[]{:S(2)}) copy-start(bf16[768,768]{1,0:T(8,128)(2,1)} %param.30) | copy-start | bytes 3538948
  12.0 6.8 %copy-start.106 = (s32[1,4]{1,0:T(1,128)S(1)}, s32[1,4]{1,0:T(1,128)}, u32[]{:S(2)}) copy-start(s32[1,4]{1,0:T(1,128)} %param.22) | copy-start | bytes 52
  12.0 7.0 %copy-start.11 = (bf16[1,256,768]{2,1,0:T(8,128)(2,1)S(1)}, bf16[1,256,768]{2,1,0:T(8,128)(2,1)}, u32[]{:S(2)}) copy-start(bf16[1,256,768]{2,1,0:T(8,128)(2,1)} %param.19) | copy-start | bytes 1179652
  12.0 48.7 %all-gather.5.cloned.1.call-start = ((), (), s32[]{:S(2)}) async-start(), calls=%async_computation.4 | async-start | bytes 1966080 | tf_op jit(solution)/shard_map/all_gather | solution.py:468
  14.8 63.3 %all-gather.11.cloned.1.call-start = ((), (), s32[]{:S(2)}) async-start(), calls=%async_computation.7 | async-start | bytes 1966080 | tf_op jit(solution)/shard_map/all_gather | solution.py:480
  17.4 82.4 %all-gather.9.cloned.1.call-start = ((), (), s32[]{:S(2)}) async-start(), calls=%async_computation.6 | async-start | bytes 1966080 | tf_op jit(solution)/shard_map/all_gather | solution.py:481
  18.7 275.1 %reduce-scatter.5.cloned.1.call-start = ((), (), s32[]{:S(2)}) async-start(), calls=%async_computation.8 | async-start | bytes 1966080 | tf_op jit(solution)/shard_map/reduce_scatter | solution.py:553
  22.8 6.1 %copy-start.67 = (s32[256,512]{0,1:T(8,128)}, s32[256,512]{0,1:T(8,128)S(1)}, u32[]{:S(2)}) copy-start(s32[256,512]{0,1:T(8,128)S(1)} %copy.113) | copy-start | bytes 1572868
  23.0 5.9 %copy-start.69 = (s32[256,512]{0,1:T(8,128)}, s32[256,512]{0,1:T(8,128)S(1)}, u32[]{:S(2)}) copy-start(s32[256,512]{0,1:T(8,128)S(1)} %copy.110) | copy-start | bytes 1572868
  28.9 6.0 %copy-start.107 = (s32[1,4]{1,0:T(1,128)S(1)}, s32[1,4]{1,0:T(1,128)}, u32[]{:S(2)}) copy-start(s32[1,4]{1,0:T(1,128)} %param.23) | copy-start | bytes 52
  28.9 6.2 %copy-start.104 = (bf16[768]{0:T(1024)(128)(2,1)S(1)}, bf16[768]{0:T(1024)(128)(2,1)}, u32[]{:S(2)}) copy-start(bf16[768]{0:T(1024)(128)(2,1)} %param.35) | copy-start | bytes 4612
  28.9 6.8 %copy-start.105 = (bf16[768]{0:T(1024)(128)(2,1)S(1)}, bf16[768]{0:T(1024)(128)(2,1)}, u32[]{:S(2)}) copy-start(bf16[768]{0:T(1024)(128)(2,1)} %param.36) | copy-start | bytes 4612
  109.4 8.6 %slice-start.6 = ((s8[6291456]{0:T(1024)(128)(4,1)}), s8[2097152]{0:T(1024)(128)(4,1)S(1)}, s32[]{:S(2)}) async-start(s8[6291456]{0:T(1024)(128)(4,1)} %bitcast.278), calls=%async_computation.18 | async-start | bytes 4194304
  111.8 6.1 %slice-start.7 = ((s8[6291456]{0:T(1024)(128)(4,1)}), s8[4194304]{0:T(1024)(128)(4,1)S(1)}, s32[]{:S(2)}) async-start(s8[6291456]{0:T(1024)(128)(4,1)} %bitcast.278), calls=%async_computation.19 | async-start | bytes 8388608
  116.4 5.1 %copy-start.2 = (f32[12,256,512]{2,1,0:T(8,128)}, f32[12,256,512]{2,1,0:T(8,128)S(1)}, u32[]{:S(2)}) copy-start(f32[12,256,512]{2,1,0:T(8,128)S(1)} %get-tuple-element.61) | copy-start | bytes 18874372
  127.0 12.9 %copy-start.8 = (f32[256,768]{1,0:T(8,128)}, f32[256,768]{1,0:T(8,128)S(1)}, u32[]{:S(2)}) copy-start(f32[256,768]{1,0:T(8,128)S(1)} %get-tuple-element.67) | copy-start | bytes 2359300
  130.8 6.4 %copy-start.4 = (f32[12,256,512]{2,1,0:T(8,128)}, f32[12,256,512]{2,1,0:T(8,128)S(1)}, u32[]{:S(2)}) copy-start(f32[12,256,512]{2,1,0:T(8,128)S(1)} %get-tuple-element.71) | copy-start | bytes 18874372
  139.9 10.2 %copy-start.54 = (bf16[256,12,64]{0,2,1:T(8,128)(2,1)}, bf16[256,12,64]{0,2,1:T(8,128)(2,1)S(1)}, u32[]{:S(2)}) copy-start(bf16[256,12,64]{0,2,1:T(8,128)(2,1)S(1)} %get-tuple-element.72) | copy-start | bytes 1179652
  139.9 10.2 %slice-start.10 = ((s8[4718592]{0:T(1024)(128)(4,1)}), s8[4194304]{0:T(1024)(128)(4,1)S(1)}, s32[]{:S(2)}) async-start(s8[4718592]{0:T(1024)(128)(4,1)} %bitcast.354), calls=%async_computation.22 | async-start | bytes 8388608
  140.5 13.9 %copy-start.25 = (f32[256,768]{1,0:T(8,128)}, f32[256,768]{1,0:T(8,128)S(1)}, u32[]{:S(2)}) copy-start(f32[256,768]{1,0:T(8,128)S(1)} %get-tuple-element.75) | copy-start | bytes 2359300
  140.5 13.9 %copy-start.96 = (f32[256]{0:T(256)}, f32[256]{0:T(256)S(1)}, u32[]{:S(2)}) copy-start(f32[256]{0:T(256)S(1)} %fusion.107) | copy-start | bytes 3076
  140.6 9.6 %copy-start.71 = (bf16[1,256,768]{2,1,0:T(8,128)(2,1)S(1)}, bf16[1,256,768]{2,1,0:T(8,128)(2,1)}, u32[]{:S(2)}) copy-start(bf16[1,256,768]{2,1,0:T(8,128)(2,1)} %param.21) | copy-start | bytes 1179652
  140.6 9.6 %slice-start.11 = ((s8[4718592]{0:T(1024)(128)(4,1)}), s8[524288]{0:T(1024)(128)(4,1)S(1)}, s32[]{:S(2)}) async-start(s8[4718592]{0:T(1024)(128)(4,1)} %bitcast.354), calls=%async_computation.23 | async-start | bytes 1048576
  156.9 8.0 %slice-start.2 = ((s8[6291456]{0:T(1024)(128)(4,1)}), s8[2097152]{0:T(1024)(128)(4,1)S(1)}, s32[]{:S(2)}) async-start(s8[6291456]{0:T(1024)(128)(4,1)} %bitcast.272), calls=%async_computation.14 | async-start | bytes 4194304
  160.3 4.7 copy-start.66
  160.3 4.7 copy-start.81
  172.7 6.1 %slice-start = ((s8[6291456]{0:T(1024)(128)(4,1)}), s8[2097152]{0:T(1024)(128)(4,1)S(1)}, s32[]{:S(2)}) async-start(s8[6291456]{0:T(1024)(128)(4,1)} %bitcast.270), calls=%async_computation.12 | async-start | bytes 4194304
  184.1 112.6 %reduce-scatter.7.cloned.1.call-start = ((), (), s32[]{:S(2)}) async-start(), calls=%async_computation.9 | async-start | bytes 1966080 | tf_op jit(solution)/shard_map/reduce_scatter | solution.py:556
  193.8 108.6 %reduce-scatter.9.cloned.1.call-start = ((), (), s32[]{:S(2)}) async-start(), calls=%async_computation.10 | async-start | bytes 1966080 | tf_op jit(solution)/shard_map/reduce_scatter | solution.py:518
  196.5 9.4 %slice-start.4 = ((s8[6291456]{0:T(1024)(128)(4,1)}), s8[2097152]{0:T(1024)(128)(4,1)S(1)}, s32[]{:S(2)}) async-start(s8[6291456]{0:T(1024)(128)(4,1)} %bitcast.274), calls=%async_computation.16 | async-start | bytes 4194304
  200.6 5.3 %slice-start.5 = ((s8[6291456]{0:T(1024)(128)(4,1)}), s8[4194304]{0:T(1024)(128)(4,1)S(1)}, s32[]{:S(2)}) async-start(s8[6291456]{0:T(1024)(128)(4,1)} %bitcast.274), calls=%async_computation.17 | async-start | bytes 8388608
  208.4 96.8 %reduce-scatter.11.cloned.1.call-start = ((), (), s32[]{:S(2)}) async-start(), calls=%async_computation.11 | async-start | bytes 1966080 | tf_op jit(solution)/shard_map/reduce_scatter | solution.py:521
  244.2 5.4 %copy-start.61 = (bf16[12,64,512]{2,1,0:T(8,128)(2,1)S(1)}, bf16[12,64,512]{2,1,0:T(8,128)(2,1)}, u32[]{:S(2)}) copy-start(bf16[12,64,512]{2,1,0:T(8,128)(2,1)} %convolution_convert_fusion.10) | copy-start | bytes 2359300
  244.3 5.4 %copy-start.62 = (bf16[12,64,512]{2,1,0:T(8,128)(2,1)S(1)}, bf16[12,64,512]{2,1,0:T(8,128)(2,1)}, u32[]{:S(2)}) copy-start(bf16[12,64,512]{2,1,0:T(8,128)(2,1)} %convolution_convert_fusion.11) | copy-start | bytes 2359300
  274.1 10.5 %copy-start.17 = (f32[256,768]{1,0:T(8,128)S(1)}, f32[256,768]{1,0:T(8,128)}, u32[]{:S(2)}) copy-start(f32[256,768]{1,0:T(8,128)} %copy-done.16) | copy-start | bytes 2359300
  274.1 10.5 %copy-start.53 = (bf16[256,12,64]{0,2,1:T(8,128)(2,1)S(1)}, bf16[256,12,64]{0,2,1:T(8,128)(2,1)}, u32[]{:S(2)}) copy-start(bf16[256,12,64]{0,2,1:T(8,128)(2,1)} %copy-done.52) | copy-start | bytes 1179652
  279.0 8.2 %copy-start.10 = (f32[256,768]{1,0:T(8,128)S(1)}, f32[256,768]{1,0:T(8,128)}, u32[]{:S(2)}) copy-start(f32[256,768]{1,0:T(8,128)} %copy-done.8) | copy-start | bytes 2359300
  279.0 8.2 %copy-start.89 = (f32[768]{0:T(1024)S(1)}, f32[768]{0:T(1024)}, u32[]{:S(2)}) copy-start(f32[768]{0:T(1024)} %convert_element_type.579) | copy-start | bytes 9220
  279.0 8.2 %copy-start.94 = (f32[256]{0:T(256)S(1)}, f32[256]{0:T(256)}, u32[]{:S(2)}) copy-start(f32[256]{0:T(256)} %copy-done.92) | copy-start | bytes 3076
  288.9 4.9 %copy-start.64 = (f32[256,768]{1,0:T(8,128)S(1)}, f32[256,768]{1,0:T(8,128)}, u32[]{:S(2)}) copy-start(f32[256,768]{1,0:T(8,128)} %fusion.132) | copy-start | bytes 2359300
  293.8 6.6 %copy-start.98 = (f32[1,4,192]{2,1,0:T(4,128)S(1)}, f32[1,4,192]{2,1,0:T(4,128)}, u32[]{:S(2)}) copy-start(f32[1,4,192]{2,1,0:T(4,128)} %stack.14) | copy-start | bytes 9220
  293.8 8.6 %copy-start.39 = (bf16[1,256,768]{2,1,0:T(8,128)(2,1)S(1)}, bf16[1,256,768]{2,1,0:T(8,128)(2,1)}, u32[]{:S(2)}) copy-start(bf16[1,256,768]{2,1,0:T(8,128)(2,1)} %param.20) | copy-start | bytes 1179652
  459.5 5.6 %copy-start.46 = (bf16[3072,768]{1,0:T(8,128)(2,1)S(1)}, bf16[3072,768]{1,0:T(8,128)(2,1)}, u32[]{:S(2)}) copy-start(bf16[3072,768]{1,0:T(8,128)(2,1)} %get-tuple-element.19) | copy-start | bytes 14155780
  (80 other events, 201.8 us)
Sparse Core Ops, SparseCore 0:
  12.1 22.4 all-gather.6
  36.7 19.5 all-gather.4
  58.4 19.6 all-gather.10
  80.1 19.6 all-gather.8
  184.2 28.1 reduce-scatter.4
  214.9 28.1 reduce-scatter.6
  245.7 28.1 reduce-scatter.8
  276.5 28.1 reduce-scatter.10

commit v2 on v0

v2 whole, which is shorter than its diff:
```python
import functools
import math
from types import SimpleNamespace

import jax
import jax.numpy as jnp
from jax import lax
from jax.experimental import pallas as pl
from jax.experimental.pallas import tpu as pltpu
from jax.sharding import PartitionSpec as P

MESH = pl.DeviceIdType.MESH
EPS = 1e-06
NEG = -1000000000.0
NEAR = 128
F32 = jnp.float32
LOW = jnp.bfloat16


def dot(left, right):
    return jnp.dot(left, right, preferred_element_type=F32)


def dot_nt(left, right):
    return lax.dot_general(left, right, (((1,), (1,)), ((), ())), preferred_element_type=F32)


def add_low(left, right):
    return (left.astype(F32) + right.astype(F32)).astype(LOW)


def block(index, size):
    return pl.ds(pl.multiple_of(index * size, size), size)


def bucket_of(distance):
    farther = jnp.full(distance.shape, 16, jnp.int32)
    for level in range(1, 16):
        farther = farther + (distance >= math.ceil(16 * 8 ** (level / 16))).astype(jnp.int32)
    return jnp.where(distance < 16, distance, farther)


def bucket_terms(buckets):
    shape = (buckets, 2 * NEAR)
    lanes = lax.broadcasted_iota(jnp.int32, shape, 1)
    return (bucket_of(lanes) == lax.broadcasted_iota(jnp.int32, shape, 0)).astype(F32)


def scale_of(values):
    return lax.rsqrt(jnp.mean(values * values, axis=-1, keepdims=True) + EPS)


def norm_back(values, gain, grad):
    scale = scale_of(values)
    gain_grad = jnp.sum(grad * values * scale, axis=0, keepdims=True)
    inner = jnp.mean(values * gain * grad, axis=-1, keepdims=True)
    return scale * gain * grad - values * (scale * scale * scale) * inner, gain_grad


def head_blocks(pair):
    size = pair.shape[0] // 2
    zero = jnp.zeros((size, pair.shape[1]), pair.dtype)
    return jnp.concatenate(
        [
            jnp.concatenate([pair[:size], zero], axis=1),
            jnp.concatenate([zero, pair[size:]], axis=1),
        ],
        axis=0,
    )


def head_rows(both):
    size, count = both.shape[0] // 2, both.shape[1] // 2
    return jnp.concatenate([both[:size, :count], both[size:, count:]], axis=0)


def twice(values):
    return jnp.concatenate([values, values], axis=1)


def fold(values):
    return values.reshape(values.shape[0] // 8, 8, values.shape[1])


class Mesh2:
    def __init__(self):
        self.row = lax.axis_index("dp")
        self.place = lax.axis_index("seq")
        self.side, self.core = self.place // 2, lax.rem(self.place, 2)
        self.sibling = self.side * 2 + 1 - self.core
        self.across = (1 - self.side) * 2 + self.core
        self.diagonal = (1 - self.side) * 2 + 1 - self.core
        self.core_peer = (self.row, self.sibling)
        self.y_peer = (self.row, self.across)

    def greet(self, peers):
        barrier = pltpu.get_barrier_semaphore()
        for peer in peers:
            pl.semaphore_signal(barrier, inc=1, device_id=peer, device_id_type=MESH)
        pl.semaphore_wait(barrier, len(peers))


def send(src, dst, sems, slot, peer):
    return pltpu.make_async_remote_copy(
        src_ref=src,
        dst_ref=dst,
        send_sem=sems.at[(0, *slot)],
        recv_sem=sems.at[(1, *slot)],
        device_id=peer,
        device_id_type=MESH,
    )


def softmax_pair(pair, r, count, steps, keys, turned, terms, queries_t, masses, out_t, probs, place):
    lanes = block(pair, 2 * r.head_dim)
    queries = head_blocks(queries_t[lanes, :])
    near = place is not None
    if near:
        tiles = [
            pltpu.roll(
                jnp.broadcast_to(r.near_bias[pl.ds(pair * 2 + head, 1), :], (NEAR, 2 * NEAR)),
                0,
                1,
                stride=1,
                stride_axis=0,
            )
            for head in range(2)
        ]
        below = [tile[:, NEAR:] for tile in tiles]
        on = [tile[:, :NEAR] for tile in tiles]
        none = jnp.zeros((NEAR, NEAR), F32)
        before = jnp.concatenate([below[0], none, below[1], none], axis=1)
        first = jnp.concatenate([on[0], below[0], on[1], below[1]], axis=1)
        second = jnp.concatenate([none, on[0], none, on[1]], axis=1)

    def score(index, top):
        rows = block(index, count)
        raw = dot(keys[rows, lanes], queries) + twice(terms[rows, :])
        r.scores[rows, :] = raw
        return jnp.maximum(top, jnp.max(fold(raw), axis=0))

    top = jnp.full((8, 2 * count), -jnp.inf, F32)
    if near:
        def score_far(index, carry):
            rows = block(index, count)
            r.scores[rows, :] = dot(keys[rows, lanes], queries) + twice(terms[rows, :])
            return carry

        lax.fori_loop(0, place, score_far, 0)
        rows = block(place, count)
        raw = dot(keys[rows, lanes], queries) + twice(terms[rows, :])
        raw = raw + jnp.concatenate([first, second], axis=0)
        r.scores[rows, :] = raw
        top = jnp.maximum(top, jnp.max(fold(raw), axis=0))

        @pl.when(place > 0)
        def _():
            last = block(place * (count // NEAR) - 1, NEAR)
            r.scores[last, :] = r.scores[last, :] + before

        def raise_top(index, top):
            return jnp.maximum(top, jnp.max(fold(r.scores[block(index, count), :]), axis=0))

        top = lax.fori_loop(0, place, raise_top, top)
    else:
        for index in range(steps):
            top = score(index, top)
    top = jnp.max(top, axis=0, keepdims=True)

    def weigh(index, carry):
        mass, context = carry
        rows = block(index, count)
        weights = jnp.exp(r.scores[rows, :] - top)
        low = weights.astype(LOW)
        probs[rows, :] = low
        context = context + dot(turned[lanes, rows], low)
        return mass + jnp.sum(fold(weights), axis=0), context

    carry = (
        jnp.zeros((8, 2 * count), F32),
        jnp.zeros((2 * r.head_dim, 2 * count), F32),
    )
    if near:
        mass, context = lax.fori_loop(0, place + 1, weigh, carry)
    else:
        for index in range(steps):
            carry = weigh(index, carry)
        mass, context = carry
    inverse = 1.0 / jnp.sum(mass, axis=0, keepdims=True)
    masses[pair] = inverse
    out_t[lanes, :] = head_rows(context * inverse)


def forward_kernel(names, dims, *refs):
    r = SimpleNamespace(**dict(zip(names, refs)), head_dim=dims.head_dim)
    m = Mesh2()
    count, places, pairs, fan, width = dims.count, dims.places, dims.pairs, dims.fan, dims.width
    q_place = m.place

    def load(slot, src, dst):
        copy = pltpu.make_async_copy(src, dst, r.load_sem.at[slot])
        copy.start()
        return copy

    loads = SimpleNamespace(
        wk=load(0, r.wk_hbm, r.wk),
        wv=load(1, r.wv_hbm, r.wv),
        wq=load(2, r.wq_hbm, r.wq),
        wout=load(3, r.wout_hbm, r.wout),
        cwk=load(4, r.cwk_hbm, r.cwk),
        cwv=load(5, r.cwv_hbm, r.cwv),
        wo=load(6, r.wo_hbm, r.wo),
        cwq=load(7, r.cwq_hbm, r.cwq),
        cwo=load(8, r.cwo_hbm, r.cwo),
        win=load(9, r.win_hbm, r.win),
    )

    m.greet([m.core_peer, m.y_peer])
    x_y = send(r.x, r.xs.at[m.place], r.link_sem, (0,), m.y_peer)
    x_core = send(r.x, r.xs.at[m.place], r.link_sem, (1,), m.core_peer)
    x_on = send(r.xs.at[m.across], r.xs.at[m.across], r.link_sem, (2,), m.core_peer)
    e_y = send(r.e, r.es.at[m.place], r.link_sem, (3,), m.y_peer)
    e_core = send(r.e, r.es.at[m.place], r.link_sem, (4,), m.core_peer)
    e_on = send(r.es.at[m.across], r.es.at[m.across], r.link_sem, (5,), m.core_peer)
    x_y.start()
    x_core.start()
    e_core.start()
    r.xs[m.place] = r.x[...]
    r.es[m.place] = r.e[...]

    gain_self = r.gain_self[...].astype(F32)
    gain_cross = r.gain_cross[...].astype(F32)
    gain_ffn = r.gain_ffn[...].astype(F32)

    items = dims.items
    dec_starts, enc_starts = [0], [0]
    for index in range(items):
        dec_starts.append(dec_starts[-1] + r.dec_len[0, index])
        enc_starts.append(enc_starts[-1] + r.enc_len[0, index])
    query_at = q_place * count + lax.broadcasted_iota(jnp.int32, (1, count), 1)
    low_self = jnp.zeros((1, count), jnp.int32)
    low_cross = jnp.zeros((1, count), jnp.int32)
    high_cross = jnp.full((1, count), enc_starts[1], jnp.int32)
    for index in range(1, items):
        inside = query_at >= dec_starts[index]
        low_self = jnp.where(inside, dec_starts[index], low_self)
        low_cross = jnp.where(inside, enc_starts[index], low_cross)
        high_cross = jnp.where(inside, enc_starts[index + 1], high_cross)

    def masks(index, carry):
        rows = block(index, count)
        key_at = index * count + lax.broadcasted_iota(jnp.int32, (count, count), 0)
        r.self_terms[rows, :] = jnp.where((key_at >= low_self) & (key_at <= query_at), 0.0, NEG)
        r.cross_terms[rows, :] = jnp.where((key_at >= low_cross) & (key_at < high_cross), 0.0, NEG)
        return carry

    lax.fori_loop(0, places, masks, 0)

    buckets = r.table.shape[0]
    terms = bucket_terms(buckets)
    last = lax.broadcasted_iota(jnp.int32, terms.shape, 0) == buckets - 1
    terms = terms - last.astype(F32)
    r.near_bias[...] = lax.dot_general(
        r.table[...], terms.astype(LOW), (((0,), (0,)), ((), ())), preferred_element_type=F32
    )

    def self_block(place):
        rows = block(place, count)
        states = r.xs[place].astype(F32)
        normed = (states * scale_of(states) * gain_self).astype(LOW)
        r.a1[rows, :] = normed
        r.keys[rows, :] = dot(normed, r.wk[...]).astype(LOW)
        values = dot(normed, r.wv[...]).astype(LOW)
        r.values[rows, :] = values
        r.values_t[:, rows] = jnp.transpose(values)

    def cross_block(place):
        rows = block(place, count)
        encoded = r.es[place]
        r.ckeys[rows, :] = dot(encoded, r.cwk[...]).astype(LOW)
        values = dot(encoded, r.cwv[...]).astype(LOW)
        r.cvalues[rows, :] = values
        r.cvalues_t[:, rows] = jnp.transpose(values)

    loads.wk.wait()
    loads.wv.wait()
    self_block(m.place)
    loads.wq.wait()
    r.queries_t[...] = jnp.transpose(dot(r.a1[block(m.place, count), :], r.wq[...]).astype(LOW))
    x_core.wait()
    self_block(m.sibling)
    loads.wout.wait()
    cotangent = r.go[...]

    def inner_grad(index, carry):
        r.inner_grad[index] = dot_nt(cotangent, r.wout[block(index, width), :])
        return carry

    lax.fori_loop(0, fan, inner_grad, 0)
    loads.cwk.wait()
    loads.cwv.wait()
    cross_block(m.place)
    e_core.wait()
    cross_block(m.sibling)
    x_y.wait()
    x_on.start()
    e_y.start()
    self_block(m.across)
    x_on.wait()
    self_block(m.diagonal)

    def keep(src, dst, slot):
        copy = pltpu.make_async_copy(src, dst, r.keep_sem.at[slot])
        copy.start()
        return copy

    kept = [
        keep(r.keys, r.keys_out, 0),
        keep(r.values, r.values_out, 1),
        keep(r.a1, r.a1_out, 2),
    ]

    def probs_copy(slot, out, pair):
        return pltpu.make_async_copy(r.probs.at[slot], out.at[pair], r.probs_sem.at[slot])

    def attend(first, last, earlier, steps, keys, turned, terms, queries_t, masses, out_t, out, place):
        def one(pair, carry):
            slot = lax.rem(pair, 2)
            if earlier:
                probs_copy(slot, out, pair).wait()
            else:
                @pl.when(pair >= 2)
                def _():
                    probs_copy(slot, out, pair).wait()
            softmax_pair(
                pair, r, count, steps, keys, turned, terms, queries_t, masses, out_t,
                r.probs.at[slot], place,
            )
            probs_copy(slot, out, pair).start()
            return carry

        lax.fori_loop(first, last, one, 0)

    split = pairs - 2
    attend(
        0, split, False, places, r.keys, r.values_t, r.self_terms, r.queries_t,
        r.self_masses, r.context_t, r.self_probs, q_place,
    )
    e_y.wait()
    e_on.start()
    attend(
        split, pairs, split >= 2, places, r.keys, r.values_t, r.self_terms, r.queries_t,
        r.self_masses, r.context_t, r.self_probs, q_place,
    )
    loads.wo.wait()
    context = jnp.transpose(r.context_t[...]).astype(LOW)
    first = r.x[...].astype(F32) + dot(context, r.wo[...])
    r.first[...] = first
    normed_cross = (first * scale_of(first) * gain_cross).astype(LOW)
    r.a2[...] = normed_cross
    loads.cwq.wait()
    r.cqueries_t[...] = jnp.transpose(dot(normed_cross, r.cwq[...]).astype(LOW))
    cross_block(m.across)
    e_on.wait()
    cross_block(m.diagonal)
    kept += [
        keep(r.ckeys, r.ckeys_out, 3),
        keep(r.cvalues, r.cvalues_out, 4),
        keep(r.es, r.es_out, 5),
    ]
    attend(
        0, pairs, True, places, r.ckeys, r.cvalues_t, r.cross_terms, r.cqueries_t,
        r.cross_masses, r.ccontext_t, r.cross_probs, None,
    )
    loads.cwo.wait()
    context = jnp.transpose(r.ccontext_t[...]).astype(LOW)
    second = r.first[...] + dot(context, r.cwo[...])
    normed_ffn = (second * scale_of(second) * gain_ffn).astype(LOW)
    r.a3[...] = normed_ffn
    r.a3_t[...] = jnp.transpose(normed_ffn)
    r.total[...] = second
    r.back[...] = jnp.zeros_like(second)
    loads.win.wait()

    own = width // places

    def head_copy(slot, index):
        side, core = index // 2, lax.rem(index, 2)
        return pltpu.make_async_copy(
            r.head_stage.at[slot], r.big.at[core, side, pl.ds(0, width)], r.head_sem.at[slot]
        )

    def tail_copy(slot, index):
        rows = pl.ds(pl.multiple_of(width + index * own, own), own)
        return pltpu.make_async_copy(
            r.tail_stage.at[slot], r.big.at[:, :, rows], r.tail_sem.at[slot]
        )

    def feed(index, carry):
        slot = lax.rem(index, 2)
        cols = block(index, width)
        pre = dot(r.a3[...], r.win[:, cols])
        half = 0.5 + 0.5 * lax.erf(pre * (0.5**0.5))
        inner = (pre * half).astype(LOW)
        slope = half + pre * jnp.exp(-0.5 * pre * pre) * ((2.0 * math.pi) ** -0.5)
        pre_grad = (slope * r.inner_grad[index]).astype(LOW)
        r.total[...] += dot(inner, r.wout[block(index, width), :])
        r.back[...] += dot_nt(pre_grad, r.win[:, cols])

        @pl.when(index >= 2)
        def _():
            head_copy(slot, index).wait()
            tail_copy(slot, index).wait()

        r.head_stage[slot] = dot(jnp.transpose(inner), r.go[...]).astype(LOW)
        grad = dot(r.a3_t[...], pre_grad).astype(LOW)
        for place in range(places):
            r.tail_stage[slot, place % 2, place // 2] = grad[place * own : (place + 1) * own]
        head_copy(slot, index).start()
        tail_copy(slot, index).start()
        return carry

    lax.fori_loop(0, fan, feed, 0)
    r.layer_out[...] = r.total[...].astype(LOW)
    second_part, gain_grad = norm_back(second, gain_ffn, r.back[...])
    r.second_grad[...] = r.go[...].astype(F32) + second_part
    r.gain_ffn_grad[...] = gain_grad
    for slot in range(2):
        probs_copy(slot, r.cross_probs, pairs - 2 + slot).wait()
        head_copy(slot, fan - 2 + slot).wait()
        tail_copy(slot, fan - 2 + slot).wait()
    for copy in kept:
        copy.wait()


def call(kernel, name, collective, limit, inputs, outputs, scratch, aliases=None):
    names = (*inputs, *outputs, *scratch)
    results = pl.pallas_call(
        functools.partial(kernel, names),
        out_shape=tuple(jax.ShapeDtypeStruct(shape, kind) for shape, kind, _ in outputs.values()),
        in_specs=[pl.BlockSpec(memory_space=space) for _, space in inputs.values()],
        out_specs=tuple(pl.BlockSpec(memory_space=space) for _, _, space in outputs.values()),
        scratch_shapes=list(scratch.values()),
        input_output_aliases=aliases or {},
        compiler_params=pltpu.CompilerParams(
            collective_id=collective, has_side_effects=True, vmem_limit_bytes=limit * 2**20
        ),
        name=name,
    )(*(array for array, _ in inputs.values()))
    return SimpleNamespace(**dict(zip(outputs, results)))


def run_forward(dims, a):
    count, total, width = dims.count, dims.count * dims.places, dims.width
    near, far, scalars = pltpu.VMEM, pl.ANY, pltpu.SMEM
    pairs, fan = dims.pairs, dims.fan
    square = (width, width)
    own = (count, width)
    inputs = dict(
        x=(a.dec_states[0], near),
        e=(a.enc_states[0], near),
        go=(a.out_grad[0], near),
        dec_len=(a.dec_lengths, scalars),
        enc_len=(a.enc_lengths, scalars),
        table=(a.position_bias, near),
        gain_self=(a.gain_self[None], near),
        gain_cross=(a.gain_cross[None], near),
        gain_ffn=(a.gain_ffn[None], near),
        wk_hbm=(a.self_key, far),
        wv_hbm=(a.self_value, far),
        wq_hbm=(a.self_query, far),
        wout_hbm=(a.ffn_out, far),
        cwk_hbm=(a.cross_key, far),
        cwv_hbm=(a.cross_value, far),
        wo_hbm=(a.self_output, far),
        cwq_hbm=(a.cross_query, far),
        cwo_hbm=(a.cross_output, far),
        win_hbm=(a.ffn_in, far),
    )
    outputs = dict(
        layer_out=(own, LOW, near),
        first=(own, F32, near),
        second_grad=(own, F32, near),
        gain_ffn_grad=((1, width), F32, near),
        queries_t=((width, count), LOW, near),
        cqueries_t=((width, count), LOW, near),
        context_t=((width, count), F32, near),
        ccontext_t=((width, count), F32, near),
        self_masses=((pairs, 1, 2 * count), F32, near),
        cross_masses=((pairs, 1, 2 * count), F32, near),
        a2=(own, LOW, near),
        keys_out=((total, width), LOW, far),
        values_out=((total, width), LOW, far),
        a1_out=((total, width), LOW, far),
        ckeys_out=((total, width), LOW, far),
        cvalues_out=((total, width), LOW, far),
        es_out=((dims.places, *own), LOW, far),
        self_probs=((pairs, total, 2 * count), LOW, far),
        cross_probs=((pairs, total, 2 * count), LOW, far),
        big=((2, 2, 4 * width, width), LOW, far),
    )
    scratch = dict(
        xs=pltpu.VMEM((dims.places, *own), LOW),
        es=pltpu.VMEM((dims.places, *own), LOW),
        wk=pltpu.VMEM(square, LOW),
        wv=pltpu.VMEM(square, LOW),
        wq=pltpu.VMEM(square, LOW),
        wout=pltpu.VMEM((fan * width, width), LOW),
        cwk=pltpu.VMEM(square, LOW),
        cwv=pltpu.VMEM(square, LOW),
        wo=pltpu.VMEM(square, LOW),
        cwq=pltpu.VMEM(square, LOW),
        cwo=pltpu.VMEM(square, LOW),
        win=pltpu.VMEM((width, fan * width), LOW),
        a1=pltpu.VMEM((total, width), LOW),
        keys=pltpu.VMEM((total, width), LOW),
        values=pltpu.VMEM((total, width), LOW),
        values_t=pltpu.VMEM((width, total), LOW),
        ckeys=pltpu.VMEM((total, width), LOW),
        cvalues=pltpu.VMEM((total, width), LOW),
        cvalues_t=pltpu.VMEM((width, total), LOW),
        self_terms=pltpu.VMEM((total, count), F32),
        cross_terms=pltpu.VMEM((total, count), F32),
        near_bias=pltpu.VMEM((dims.heads, 2 * NEAR), F32),
        scores=pltpu.VMEM((total, 2 * count), F32),
        probs=pltpu.VMEM((2, total, 2 * count), LOW),
        inner_grad=pltpu.VMEM((fan, count, width), F32),
        a3=pltpu.VMEM(own, LOW),
        a3_t=pltpu.VMEM((width, count), LOW),
        total=pltpu.VMEM(own, F32),
        back=pltpu.VMEM(own, F32),
        head_stage=pltpu.VMEM((2, width, width), LOW),
        tail_stage=pltpu.VMEM((2, 2, 2, width // dims.places, width), LOW),
        load_sem=pltpu.SemaphoreType.DMA((10,)),
        link_sem=pltpu.SemaphoreType.DMA((2, 6)),
        keep_sem=pltpu.SemaphoreType.DMA((6,)),
        probs_sem=pltpu.SemaphoreType.DMA((2,)),
        head_sem=pltpu.SemaphoreType.DMA((2,)),
        tail_sem=pltpu.SemaphoreType.DMA((2,)),
    )
    return call(
        lambda names, *refs: forward_kernel(names, dims, *refs),
        "forward", 0, 60, inputs, outputs, scratch,
    )


class Reducer:
    LAG = 10

    def __init__(self, r, m, dims):
        self.r, self.m = r, m
        self.planes = dims.planes
        self.piece = dims.piece
        self.half_rows = self.piece * self.planes
        self.chunk_rows = 2 * self.half_rows
        self.chunks = dims.chunks
        self.ring = dims.ring
        self.plane, self.half = m.row // 2, lax.rem(m.row, 2)
        self.x_peer = (self.plane * 2 + 1 - self.half, m.place)
        self.published = 0
        self.done = 0

    def z_peer(self, step):
        return (lax.rem(self.plane + step, self.planes) * 2 + self.half, self.m.place)

    def peers(self):
        return [self.x_peer] + [self.z_peer(step) for step in range(1, self.planes)]

    def span(self, first, size):
        return pl.ds(pl.multiple_of(first, self.piece), size)

    def rows(self, index):
        return self.span(index * self.chunk_rows, self.chunk_rows)

    def kept_rows(self, index, first=0, size=None):
        slot = lax.rem(index, self.ring)
        return self.span(slot * self.chunk_rows + first, size or self.chunk_rows)

    def load(self, index):
        r = self.r
        return pltpu.make_async_copy(
            r.big.at[self.m.core, :, self.rows(index)],
            r.kept.at[:, self.kept_rows(index)],
            r.chunk_sem.at[index],
        )

    def core_copy(self, index):
        r, rows = self.r, self.rows(index)
        return send(
            r.big.at[1 - self.m.core, :, rows], r.core_recv.at[:, rows], r.core_sem, (index,),
            self.m.core_peer,
        )

    def y_copy(self, index):
        r = self.r
        return send(
            r.kept.at[1 - self.m.side, self.kept_rows(index)], r.fin.at[self.rows(index)],
            r.y_sem, (index,), self.m.y_peer,
        )

    def x_copy(self, index):
        r = self.r
        other = self.kept_rows(index, (1 - self.half) * self.half_rows, self.half_rows)
        return send(
            r.kept.at[self.m.side, other],
            r.x_recv.at[self.span(index * self.half_rows, self.half_rows)],
            r.x_sem, (index,), self.x_peer,
        )

    def z_first(self, which):
        return self.half * self.half_rows + which * self.piece

    def z_copy(self, index, step):
        r = self.r
        target = lax.rem(self.plane + step, self.planes)
        return send(
            r.kept.at[self.m.side, self.kept_rows(index, self.z_first(target), self.piece)],
            r.z_recv.at[step - 1, self.span(index * self.piece, self.piece)],
            r.z_sem, (index, step - 1), self.z_peer(step),
        )

    def own_rows(self, index):
        return self.span(index * self.chunk_rows + self.z_first(self.plane), self.piece)

    def gz_copy(self, index, step):
        r, rows = self.r, self.own_rows(index)
        return send(r.fin.at[rows], r.fin.at[rows], r.gz_sem, (index, step - 1), self.z_peer(step))

    def gx_copy(self, index):
        r = self.r
        rows = self.span(index * self.chunk_rows + self.half * self.half_rows, self.half_rows)
        return send(r.fin.at[rows], r.fin.at[rows], r.gx_sem, (index,), self.x_peer)

    def publish(self, rows):
        last = rows // self.chunk_rows

        def begin(index, carry):
            self.core_copy(index).start()
            return carry

        def fetch(index, carry):
            self.load(index).start()
            return carry

        lax.fori_loop(self.published, last, begin, 0)
        first_load = max(self.published, 0)
        last_load = min(last, max(self.ring, self.freed() + self.ring))
        lax.fori_loop(first_load, last_load, fetch, 0)
        self.published = last
        self.loaded = last_load

    def freed(self):
        return max(0, self.done - 6)

    def tick(self, step):
        r, m, chunks = self.r, self.m, self.chunks

        @pl.when(step < chunks)
        def _():
            self.load(step).wait()
            self.core_copy(step).wait()
            rows, kept = self.rows(step), self.kept_rows(step)
            for other in range(2):
                r.kept[other, kept, :] = add_low(r.kept[other, kept, :], r.core_recv[other, rows, :])
            self.y_copy(step).start()

        @pl.when((step >= 2) & (step < chunks + 2))
        def _():
            index = step - 2
            self.y_copy(index).wait()
            kept = self.kept_rows(index)
            r.kept[m.side, kept, :] = add_low(r.kept[m.side, kept, :], r.fin[self.rows(index), :])
            self.x_copy(index).start()

        @pl.when((step >= 4) & (step < chunks + 4))
        def _():
            index = step - 4
            self.x_copy(index).wait()
            kept = self.kept_rows(index, self.half * self.half_rows, self.half_rows)
            arrived = r.x_recv[self.span(index * self.half_rows, self.half_rows), :]
            r.kept[m.side, kept, :] = add_low(r.kept[m.side, kept, :], arrived)
            for plane in range(1, self.planes):
                self.z_copy(index, plane).start()

        @pl.when((step >= 6) & (step < chunks + 6))
        def _():
            index = step - 6
            kept = self.kept_rows(index, self.z_first(self.plane), self.piece)
            total = r.kept[m.side, kept, :].astype(F32)
            for plane in range(1, self.planes):
                self.z_copy(index, plane).wait()
                arrived = r.z_recv[plane - 1, self.span(index * self.piece, self.piece), :]
                total = total + arrived.astype(F32)
            r.fin[self.own_rows(index), :] = total.astype(LOW)
            for plane in range(1, self.planes):
                self.gz_copy(index, plane).start()

        @pl.when((step >= 8) & (step < chunks + 8))
        def _():
            index = step - 8
            for plane in range(1, self.planes):
                self.gz_copy(index, plane).wait()
            self.gx_copy(index).start()

        @pl.when(step >= 10)
        def _():
            self.gx_copy(step - 10).wait()

    def fetch_next(self, step, limit):
        index = step - 6 + self.ring

        @pl.when((step >= 6) & (index >= self.loaded) & (index < limit))
        def _():
            self.load(index).start()

    def run(self, ticks):
        first = self.done

        def one(step, carry):
            self.tick(step)
            self.fetch_next(step, self.published)
            return carry

        lax.fori_loop(first, first + ticks, one, 0)
        self.advance(ticks)

    def advance(self, ticks):
        self.done += ticks
        self.loaded = max(self.loaded, min(self.published, self.freed() + self.ring))

    def ready(self):
        if self.published == self.chunks:
            return self.chunks + self.LAG - self.done
        return self.published - self.done

    def beside(self, loops):
        first, ticks = self.done, min(loops, self.ready())

        def one(index):
            @pl.when(index < ticks)
            def _():
                self.tick(first + index)
                self.fetch_next(first + index, self.published)

        def after():
            self.advance(ticks)

        return one, after


def attend_back(pair, r, count, keys, keys_t, values, queries_t, masses, context_t, grad_t, probs, place, places):
    lanes = block(pair, 2 * r.head_dim)
    inverse = masses[pair]
    grads = grad_t[lanes, :].astype(F32)
    product = grads * context_t[lanes, :]
    sums = [
        jnp.sum(product[: r.head_dim], axis=0, keepdims=True),
        jnp.sum(product[r.head_dim :], axis=0, keepdims=True),
    ]
    inner = jnp.concatenate(sums, axis=1) * inverse
    grads = (head_blocks(grads) * inverse).astype(LOW)
    queries = head_blocks(queries_t[lanes, :])

    def one(index, total):
        rows = block(index, count)
        weights = probs[rows, :]
        score_grad = weights.astype(F32) * (dot(values[rows, lanes], grads) - inner)
        low = score_grad.astype(LOW)
        side, core = index // 2, lax.rem(index, 2)
        r.value_grad[side, core, :, lanes] = dot_nt(weights, grads).astype(LOW)
        r.key_grad[side, core, :, lanes] = dot_nt(low, queries).astype(LOW)
        return total + dot(keys_t[lanes, rows], low), score_grad

    total = jnp.zeros((2 * r.head_dim, 2 * count), F32)
    if place is None:
        for index in range(places):
            total, _ = one(index, total)
    else:
        r.before[...] = jnp.zeros_like(r.before)

        def far(index, carry):
            total, beyond = carry
            total, score_grad = one(index, total)
            split = count - NEAR
            beyond = beyond + jnp.sum(fold(score_grad[:split]), axis=0)
            rest = score_grad[split:]
            is_last = index == place - 1

            @pl.when(is_last)
            def _():
                r.before[...] = rest

            beyond = beyond + jnp.where(is_last, 0.0, jnp.sum(fold(rest), axis=0))
            return total, beyond

        carry = (total, jnp.zeros((8, 2 * count), F32))
        total, beyond = lax.fori_loop(0, place, far, carry)
        total, own = one(place, total)
        before = r.before[...]
        parts = []
        for head in range(2):
            at = head * count
            on = own[:NEAR, at : at + NEAR] + own[NEAR:, at + NEAR : at + 2 * NEAR]
            below = before[:, at : at + NEAR] + own[:NEAR, at + NEAR : at + 2 * NEAR]
            both = jnp.concatenate([on, below], axis=1)
            summed = both[:8]
            for group in range(1, NEAR // 8):
                summed = summed + pltpu.roll(
                    both[8 * group : 8 * group + 8], 2 * NEAR - 8 * group, 1
                )
            parts.append(summed)
        summed = jnp.concatenate(parts, axis=0)
        sublane = lax.broadcasted_iota(jnp.int32, summed.shape, 0)
        for bit in (1, 2, 4):
            summed = jnp.where(
                (sublane & bit) != 0, pltpu.roll(summed, 2 * NEAR - bit, 1), summed
            )
        lane = lax.broadcasted_iota(jnp.int32, (1, 2 * NEAR), 1)
        for head in range(2):
            at = head * count
            line = jnp.sum(summed[8 * head : 8 * head + 8], axis=0, keepdims=True)
            rest = jnp.sum(beyond[:, at : at + count]) + jnp.sum(before[:, at + NEAR : at + 2 * NEAR])
            line = line + jnp.where(lane == 2 * NEAR - 1, rest, 0.0)
            r.by_distance[pl.ds(pair * 2 + head, 1), :] = line
    r.query_grad_t[lanes, :] = head_rows(total).astype(LOW)


def backward_kernel(names, dims, *refs):
    r = SimpleNamespace(**dict(zip(names, refs)), head_dim=dims.head_dim)
    m = Mesh2()
    count, places, pairs, width = dims.count, dims.places, dims.pairs, dims.width
    own = width // places
    engine = Reducer(r, m, dims)

    loads = SimpleNamespace()
    slots = iter(range(r.load_sem.shape[0]))

    def load(src, dst):
        copy = pltpu.make_async_copy(src, dst, r.load_sem.at[next(slots)])
        copy.start()
        return copy

    def probs_copy(src, pair):
        slot = lax.rem(pair, 2)
        return pltpu.make_async_copy(src.at[pair], r.probs.at[slot], r.probs_sem.at[slot])

    loads.second = load(r.second_hbm, r.dec_grad)
    loads.cwo = load(r.cwo_hbm, r.wo)
    loads.ckeys = load(r.ckeys_hbm, r.keys)
    loads.cvalues = load(r.cvalues_hbm, r.values)
    probs_copy(r.cross_probs, 0).start()
    probs_copy(r.cross_probs, 1).start()
    loads.first = load(r.first_hbm, r.enc_grad)
    loads.cwq = load(r.cwq_hbm, r.wq)
    loads.cwk = load(r.cwk_hbm, r.wk)
    loads.cwv = load(r.cwv_hbm, r.wv)
    loads.es0 = load(r.es_hbm.at[m.core], r.group.at[0])
    loads.es1 = load(r.es_hbm.at[m.core + 2], r.group.at[1])

    m.greet([m.core_peer, m.y_peer] + engine.peers())
    engine.publish(2 * width)

    gain_self = r.gain_self[...].astype(F32)
    gain_cross = r.gain_cross[...].astype(F32)
    staged = {}

    def unit_copy(unit):
        rows = pl.ds(2 * width + unit * own, own)
        return pltpu.make_async_copy(
            r.stage.at[unit % 2], r.big.at[:, :, rows], r.stage_sem.at[unit % 2]
        )

    def give(unit, left_t, right):
        if unit - 2 in staged:
            staged.pop(unit - 2).wait()
        for place in range(places):
            grad = dot(left_t[place * own : (place + 1) * own, :], right)
            r.stage[unit % 2, place % 2, place // 2] = grad.astype(LOW)
        staged[unit] = unit_copy(unit)
        staged[unit].start()

    def settle(rows):
        for unit in sorted(staged):
            staged.pop(unit).wait()
        engine.publish(rows)

    def turn(src, dst):
        def one(index, carry):
            rows = block(index, count)
            dst[:, rows] = jnp.transpose(src[rows, :])
            return carry

        lax.fori_loop(0, places, one, 0)

    def attend(src, queries_t, masses, context_t, grad_t, place):
        tick, after = engine.beside(pairs)

        def one(pair, carry):
            probs_copy(src, pair).wait()
            attend_back(
                pair, r, count, r.keys, r.keys_t, r.values, queries_t, masses, context_t, grad_t,
                r.probs.at[lax.rem(pair, 2)], place, places,
            )

            @pl.when(pair + 2 < pairs)
            def _():
                probs_copy(src, pair + 2).start()

            tick(pair)
            return carry

        lax.fori_loop(0, pairs, one, 0)
        after()

    def exchange(slot, key_recv, value_recv):
        copies = [
            send(r.key_grad.at[:, 1 - m.core], key_recv, r.link_sem, (slot,), m.core_peer),
            send(r.value_grad.at[:, 1 - m.core], value_recv, r.link_sem, (slot + 1,), m.core_peer),
        ]
        for copy in copies:
            copy.start()
        return copies

    def chip_sum(grad, arrived):
        return add_low(grad[:, m.core], arrived[...]).reshape(2 * count, width)

    def partial(slot, side):
        key_grad = add_low(r.key_grad[side, m.core], r.key_recv[slot, side])
        value_grad = add_low(r.value_grad[side, m.core], r.value_recv[slot, side])
        return dot_nt(key_grad, r.wk[...]) + dot_nt(value_grad, r.wv[...])

    loads.second.wait()
    head_grad = r.dec_grad[...].astype(LOW)
    loads.cwo.wait()
    r.grad_t[...] = dot_nt(r.wo[...], head_grad).astype(LOW)
    loads.wo = load(r.wo_hbm, r.wo)
    give(0, r.ccontext_t[...].astype(LOW), head_grad)
    loads.ckeys.wait()
    turn(r.keys, r.keys_t)
    loads.cvalues.wait()
    attend(r.cross_probs, r.cqueries_t, r.cross_masses, r.ccontext_t, r.grad_t, None)
    copies = exchange(0, r.key_recv.at[0], r.value_recv.at[0])
    loads.keys = load(r.keys_hbm, r.keys)
    loads.values = load(r.values_hbm, r.values)
    probs_copy(r.self_probs, 0).start()
    probs_copy(r.self_probs, 1).start()
    query_grad = jnp.transpose(r.query_grad_t[...])
    loads.cwq.wait()
    normed_grad = dot_nt(query_grad, r.wq[...])
    loads.wq = load(r.wq_hbm, r.wq)
    loads.first.wait()
    first_part, gain_cross_grad = norm_back(r.enc_grad[...], gain_cross, normed_grad)
    r.dec_grad[...] += first_part
    give(1, jnp.transpose(r.a2[...]), query_grad)
    loads.es0.wait()
    loads.es1.wait()
    for side in range(2):
        r.group_t[:, side * count : (side + 1) * count] = jnp.transpose(r.group[side])
    loads.a10 = load(r.a1_hbm.at[block(m.core, count)], r.group.at[0])
    loads.a11 = load(r.a1_hbm.at[block(m.core + 2, count)], r.group.at[1])
    for copy in copies:
        copy.wait()
    key_grad = chip_sum(r.key_grad, r.key_recv.at[0])
    value_grad = chip_sum(r.value_grad, r.value_recv.at[0])
    loads.cwk.wait()
    loads.cwv.wait()
    r.partial_low[...] = partial(0, 1 - m.side).astype(LOW)
    enc_copy = send(r.partial_low, r.partial_recv.at[0], r.link_sem, (4,), m.y_peer)
    enc_copy.start()
    r.enc_grad[...] = partial(0, m.side)
    loads.wk = load(r.wk_hbm, r.wk)
    loads.wv = load(r.wv_hbm, r.wv)
    give(2, r.group_t[...], key_grad)
    give(3, r.group_t[...], value_grad)
    settle(3 * width)

    first_grad = r.dec_grad[...]
    head_grad = first_grad.astype(LOW)
    loads.wo.wait()
    r.grad_t[...] = dot_nt(r.wo[...], head_grad).astype(LOW)
    give(4, r.context_t[...].astype(LOW), head_grad)
    loads.keys.wait()
    turn(r.keys, r.keys_t)
    loads.values.wait()

    def clear(index, carry):
        side, core = index // 2, lax.rem(index, 2)
        r.key_grad[side, core] = jnp.zeros((count, width), LOW)
        r.value_grad[side, core] = jnp.zeros((count, width), LOW)
        return carry

    lax.fori_loop(m.place + 1, places, clear, 0)
    r.by_distance[...] = jnp.zeros_like(r.by_distance)
    attend(r.self_probs, r.queries_t, r.self_masses, r.context_t, r.grad_t, m.place)
    copies = exchange(2, r.key_recv.at[1], r.value_recv.at[1])
    query_grad = jnp.transpose(r.query_grad_t[...])
    loads.wq.wait()
    normed_grad = dot_nt(query_grad, r.wq[...])
    loads.a10.wait()
    loads.a11.wait()
    for side in range(2):
        r.group_t[:, side * count : (side + 1) * count] = jnp.transpose(r.group[side])
    give(5, jnp.transpose(r.group[m.side]), query_grad)
    for copy in copies:
        copy.wait()
    key_grad = chip_sum(r.key_grad, r.key_recv.at[1])
    value_grad = chip_sum(r.value_grad, r.value_recv.at[1])
    loads.wk.wait()
    loads.wv.wait()
    enc_copy.wait()
    r.enc_grad[...] += r.partial_recv[0].astype(F32)
    r.partial_low[...] = partial(1, 1 - m.side).astype(LOW)
    dec_copy = send(r.partial_low, r.partial_recv.at[1], r.link_sem, (5,), m.y_peer)
    dec_copy.start()
    normed_grad = normed_grad + partial(1, m.side)
    give(6, r.group_t[...], key_grad)
    give(7, r.group_t[...], value_grad)
    settle(4 * width)
    dec_copy.wait()
    normed_grad = normed_grad + r.partial_recv[1].astype(F32)
    state_part, gain_self_grad = norm_back(r.x[...].astype(F32), gain_self, normed_grad)
    r.dec_grad[...] += state_part

    buckets = dims.buckets
    table = lax.dot_general(
        bucket_terms(buckets), r.by_distance[...], (((1,), (1,)), ((), ())),
        precision=lax.Precision.HIGHEST, preferred_element_type=F32,
    )
    r.tiny[0] = jnp.zeros(r.tiny.shape[1:], F32)
    r.tiny[0, 0:1] = gain_self_grad
    r.tiny[0, 1:2] = gain_cross_grad
    r.tiny[0, 2:3] = r.gain_ffn_grad[...]
    part = buckets // places
    for place in range(places):
        r.tiny[0, 8 : 8 + part, 128 * place : 128 * (place + 1)] = table[
            place * part : (place + 1) * part
        ]
    for slot, peer in enumerate((m.core_peer, m.y_peer, engine.x_peer)):
        copy = send(r.tiny.at[slot], r.tiny_recv.at[slot], r.tiny_sem, (slot,), peer)
        copy.start()
        copy.wait()
        r.tiny[slot + 1] = r.tiny[slot] + r.tiny_recv[slot]
    copies = []
    for step in range(1, dims.planes):
        copy = send(
            r.tiny.at[3], r.tiny_recv.at[2 + step], r.tiny_sem, (2 + step,), engine.z_peer(step)
        )
        copy.start()
        copies.append(copy)
    for copy in copies:
        copy.wait()
    total = r.tiny[3]
    for step in range(1, dims.planes):
        total = total + r.tiny_recv[2 + step]
    r.small[...] = total
    engine.run(engine.ready())


def run_backward(dims, a, f):
    count, total, width = dims.count, dims.count * dims.places, dims.width
    near, far = pltpu.VMEM, pl.ANY
    pairs, planes, chunks, piece = dims.pairs, dims.planes, dims.chunks, dims.piece
    square = (width, width)
    own = (count, width)
    inputs = dict(
        x=(a.dec_states[0], near),
        gain_self=(a.gain_self[None], near),
        gain_cross=(a.gain_cross[None], near),
        first_hbm=(f.first, far),
        second_hbm=(f.second_grad, far),
        gain_ffn_grad=(f.gain_ffn_grad, near),
        queries_t=(f.queries_t, near),
        cqueries_t=(f.cqueries_t, near),
        context_t=(f.context_t, near),
        ccontext_t=(f.ccontext_t, near),
        self_masses=(f.self_masses, near),
        cross_masses=(f.cross_masses, near),
        a2=(f.a2, near),
        keys_hbm=(f.keys_out, far),
        values_hbm=(f.values_out, far),
        a1_hbm=(f.a1_out, far),
        ckeys_hbm=(f.ckeys_out, far),
        cvalues_hbm=(f.cvalues_out, far),
        es_hbm=(f.es_out, far),
        self_probs=(f.self_probs, far),
        cross_probs=(f.cross_probs, far),
        wo_hbm=(a.self_output, far),
        wq_hbm=(a.self_query, far),
        wk_hbm=(a.self_key, far),
        wv_hbm=(a.self_value, far),
        cwo_hbm=(a.cross_output, far),
        cwq_hbm=(a.cross_query, far),
        cwk_hbm=(a.cross_key, far),
        cwv_hbm=(a.cross_value, far),
        big_in=(f.big, far),
    )
    outputs = dict(
        big=(f.big.shape, LOW, far),
        fin=((4 * width, width), LOW, near),
        dec_grad=(own, F32, near),
        enc_grad=(own, F32, near),
        small=((16, width), F32, near),
    )
    dma = pltpu.SemaphoreType.DMA
    rows = 4 * width
    chunk_rows = 2 * planes * piece
    scratch = dict(
        wo=pltpu.VMEM(square, LOW),
        wq=pltpu.VMEM(square, LOW),
        wk=pltpu.VMEM(square, LOW),
        wv=pltpu.VMEM(square, LOW),
        keys=pltpu.VMEM((total, width), LOW),
        values=pltpu.VMEM((total, width), LOW),
        keys_t=pltpu.VMEM((width, total), LOW),
        probs=pltpu.VMEM((2, total, 2 * count), LOW),
        grad_t=pltpu.VMEM((width, count), LOW),
        query_grad_t=pltpu.VMEM((width, count), LOW),
        key_grad=pltpu.VMEM((2, 2, *own), LOW),
        value_grad=pltpu.VMEM((2, 2, *own), LOW),
        key_recv=pltpu.VMEM((2, 2, *own), LOW),
        value_recv=pltpu.VMEM((2, 2, *own), LOW),
        partial_low=pltpu.VMEM(own, LOW),
        partial_recv=pltpu.VMEM((2, *own), LOW),
        group=pltpu.VMEM((2, *own), LOW),
        group_t=pltpu.VMEM((width, 2 * count), LOW),
        before=pltpu.VMEM((NEAR, 2 * count), F32),
        by_distance=pltpu.VMEM((128, 2 * NEAR), F32),
        stage=pltpu.VMEM((2, 2, 2, width // dims.places, width), LOW),
        kept=pltpu.VMEM((2, dims.ring * chunk_rows, width), LOW),
        core_recv=pltpu.VMEM((2, rows, width), LOW),
        x_recv=pltpu.VMEM((rows // 2, width), LOW),
        z_recv=pltpu.VMEM((planes - 1, chunks * piece, width), LOW),
        tiny=pltpu.VMEM((4, 16, width), F32),
        tiny_recv=pltpu.VMEM((2 + planes, 16, width), F32),
        load_sem=dma((18,)),
        probs_sem=dma((2,)),
        stage_sem=dma((2,)),
        link_sem=dma((2, 6)),
        chunk_sem=dma((chunks,)),
        core_sem=dma((2, chunks)),
        y_sem=dma((2, chunks)),
        x_sem=dma((2, chunks)),
        z_sem=dma((2, chunks, planes - 1)),
        gz_sem=dma((2, chunks, planes - 1)),
        gx_sem=dma((2, chunks)),
        tiny_sem=dma((2, 2 + planes)),
    )
    return call(
        lambda names, *refs: backward_kernel(names, dims, *refs),
        "backward", 1, 63, inputs, outputs, scratch, {len(inputs) - 1: 0},
    )


def place_kernel(names, dims, *refs):
    r = SimpleNamespace(**dict(zip(names, refs)))
    width, fan = dims.width, dims.fan
    own = width // dims.places
    r.ffn_out_grad[...] = r.fin[:width].astype(F32)
    for index in range(fan):
        first = width + index * own
        r.ffn_in_grad[:, index * width : (index + 1) * width] = r.fin[first : first + own].astype(F32)
    units = (
        r.cross_output, r.cross_query, r.cross_key, r.cross_value,
        r.self_output, r.self_query, r.self_key, r.self_value,
    )
    for index, grad in enumerate(units):
        first = 2 * width + index * own
        grad[...] = r.fin[first : first + own].astype(F32)
    r.layer[...] = r.layer_in[...]
    r.dec[...] = r.dec_in[...]
    r.enc[...] = r.enc_in[...]
    at = lax.axis_index("seq")
    part = dims.buckets // dims.places
    for place in range(dims.places):
        @pl.when(at == place)
        def _():
            for index, grad in enumerate((r.gain_self, r.gain_cross, r.gain_ffn)):
                grad[...] = r.small[index : index + 1, place * own : (place + 1) * own]
            r.table_grad[...] = r.small[8 : 8 + part, 128 * place : 128 * place + dims.heads]


def run_place(dims, f, b):
    near = pltpu.VMEM
    width, own = dims.width, dims.width // dims.places
    square, gain = ((own, width), F32, near), ((1, own), F32, near)
    inputs = dict(
        fin=(b.fin, near),
        small=(b.small, near),
        layer_in=(f.layer_out, near),
        dec_in=(b.dec_grad, near),
        enc_in=(b.enc_grad, near),
    )
    outputs = dict(
        layer=(f.layer_out.shape, LOW, near),
        dec=(b.dec_grad.shape, F32, near),
        enc=(b.enc_grad.shape, F32, near),
        ffn_out_grad=((width, width), F32, near),
        ffn_in_grad=((own, dims.fan * width), F32, near),
        cross_output=square,
        cross_query=square,
        cross_key=square,
        cross_value=square,
        self_output=square,
        self_query=square,
        self_key=square,
        self_value=square,
        gain_self=gain,
        gain_cross=gain,
        gain_ffn=gain,
        table_grad=((dims.buckets // dims.places, dims.heads), F32, near),
    )
    names = (*inputs, *outputs)
    results = pl.pallas_call(
        lambda *refs: place_kernel(names, dims, *refs),
        out_shape=tuple(jax.ShapeDtypeStruct(shape, kind) for shape, kind, _ in outputs.values()),
        in_specs=[pl.BlockSpec(memory_space=space) for _, space in inputs.values()],
        out_specs=tuple(pl.BlockSpec(memory_space=space) for _, _, space in outputs.values()),
        compiler_params=pltpu.CompilerParams(vmem_limit_bytes=40 * 2**20),
        name="place",
    )(*(array for array, _ in inputs.values()))
    return SimpleNamespace(**dict(zip(outputs, results)))


def on_device(
    dec_states,
    enc_states,
    out_grad,
    dec_lengths,
    enc_lengths,
    self_query,
    self_key,
    self_value,
    self_output,
    cross_query,
    cross_key,
    cross_value,
    cross_output,
    ffn_in,
    ffn_out,
    gain_self,
    gain_cross,
    gain_ffn,
    position_bias,
):
    a = SimpleNamespace(
        dec_states=dec_states,
        enc_states=enc_states,
        out_grad=out_grad,
        dec_lengths=dec_lengths,
        enc_lengths=enc_lengths,
        self_query=self_query,
        self_key=self_key,
        self_value=self_value,
        self_output=self_output,
        cross_query=cross_query,
        cross_key=cross_key,
        cross_value=cross_value,
        cross_output=cross_output,
        ffn_in=ffn_in,
        ffn_out=ffn_out,
        gain_self=gain_self,
        gain_cross=gain_cross,
        gain_ffn=gain_ffn,
        position_bias=position_bias,
    )
    count, width = a.dec_states.shape[1:]
    buckets, heads = a.position_bias.shape
    planes, piece = lax.axis_size("dp") // 2, 16
    chunks = 4 * width // (2 * planes * piece)
    dims = SimpleNamespace(
        count=count,
        width=width,
        places=lax.axis_size("seq"),
        heads=heads,
        head_dim=width // heads,
        pairs=heads // 2,
        fan=a.ffn_in.shape[1] // width,
        items=a.dec_lengths.shape[1],
        buckets=buckets,
        planes=planes,
        piece=piece,
        chunks=chunks,
        ring=min(chunks, 12),
    )
    f = run_forward(dims, a)
    b = run_backward(dims, a, f)
    o = run_place(dims, f, b)
    return (
        o.layer[None],
        o.dec[None],
        o.enc[None],
        o.self_query,
        o.self_key,
        o.self_value,
        o.self_output,
        o.cross_query,
        o.cross_key,
        o.cross_value,
        o.cross_output,
        o.ffn_in_grad,
        o.ffn_out_grad,
        o.gain_self[0],
        o.gain_cross[0],
        o.gain_ffn[0],
        o.table_grad,
    )


def solution(mesh):
    split = P("dp", "seq", None)
    rows = P("seq", None)
    return jax.shard_map(
        on_device,
        mesh=mesh,
        in_specs=(split,) * 3 + (P("dp", None),) * 2 + (P(),) * 14,
        out_specs=(split,) * 3 + (rows,) * 10 + (P("seq"),) * 3 + (rows,),
        check_vma=False,
    )
```

time: 1020 us -> 242 us (0.24); the launches traced: 1010 us -> 242 us
  blocking collectives: 394 us -> 0 us
  waiting for transfers between devices: 339 us -> 0 us
  Pallas kernels: 0 us -> 231 us
  matrix products: 148 us -> 0 us
  local copies, waits for them, and re-layouts: 82.4 us -> 10.6 us
  other arithmetic: 25.6 us -> 0 us
  between operations: 17.4 us -> 0.7 us
    psum x1 -> x0, blocking collectives: 383 us -> none  [on_device(): lax.psum((lax.psum_scatter(grad_self_query.astype(jnp.bfloat16), 'seq', s...]
    reduce_scatter x12 -> x0, waiting for transfers between devices: 275 us -> none  [the longest x1 50.5 us: on_device(): lax.psum_scatter(grad_ffn_out.astype(jnp.bfloat16), 'seq', scatter_dimens...]
    pallas_call x0 -> x3, Pallas kernels: none -> 231 us  [the longest x2 226 us: call(): pl.pallas_call(functools.partial(kernel, names), out_shape=tuple((jax.Sha...]
    dot_general x58 -> x0, matrix products: 148 us -> none  [the longest x10 29.2 us: matmul_left_t(): lax.dot_general(left, right, (((0,), (0,)), ((), ())), preferred_element_...]
    unnamed x20 -> x0, waiting for transfers between devices: 33 us -> none
    all_gather x4 -> x0, waiting for transfers between devices: 31.7 us -> none  [the longest x1 17 us: on_device(): lax.all_gather(cross_values_own, 'seq', axis=0, tiled=True)]
    slice x16 -> x0, local copies, waits for them, and re-layouts: 23 us -> none  [the longest x6 11.9 us: block_scores(): key_block = keys_all[start:start + span].reshape(span, heads, head_dim)]
    convert_element_type x6 -> x0, local copies, waits for them, and re-layouts: 19.9 us -> none  [the longest x2 15.7 us: attention_backward(): (probs * (prob_grad - row_terms[:, :, None])).astype(jnp.bfloat16)]
  transfers between devices with their start and end apart: 18 -> 0, of which waited for: 13 -> 0; matrix products, arithmetic and copies ran while one was open for 17% -> 0% of each run, Pallas kernels for 0% -> 0%
where the time goes in v2:
time: 242 us
  Pallas kernels  231 us (95%)
  local copies, waits for them, and re-layouts  10.6 us (4%)
    pallas_call x2, Pallas kernels, call(): pl.pallas_call(functools.partial(kernel, names), out_shape=tuple((jax.Sha...  226 us
    unnamed x11, local copies, waits for them, and re-layouts  6.77 us
    pallas_call x1, Pallas kernels, run_place(): pl.pallas_call(lambda *refs: place_kernel(names, dims, *refs), out_shape=...  4.95 us

profile of v2, /device:TPU:0, one launch (start us, length us, event | category | flops | bytes accessed | tf_op | source)
XLA Modules:
  0.0 241.9 jit_solution(7846430922579721792)
XLA Ops:
  0.7 1.3 broadcast_in_dim.20.refs_6_.refs_1_
  1.9 1.3 broadcast_in_dim.21.refs_7_.refs_2_
  3.2 1.3 broadcast_in_dim.22.refs_8_
  4.4 1.4 copy.37.refs_5_
  5.8 46.7 %forward.1 = (bf16[256,768]{1,0:T(8,128)(2,1)}, f32[256,768]{1,0:T(8,128)}, f32[256,768]{1,0:T(8,128)}, f32[1,768]{1,0:T(1,128)}, bf16[768,256]{1,0:T(8,128)(2,1...) custom-call(bf16[256,768]{1,0:T(8,128)(2,1)} %bitcast.9, ...), custom_call_target="tpu_custom_call" | custom-call | tf_op jit(solution)/shard_map/forward/pallas_call | solution.py:438
  52.5 0.0 copy-start.3
  52.5 178.9 %backward.1 = (bf16[2,2,3072,768]{3,2,1,0:T(8,128)(2,1)}, bf16[3072,768]{1,0:T(8,128)(2,1)}, f32[256,768]{1,0:T(8,128)}, f32[256,768]{1,0:T(8,128)}, f32[16,768]{1,0:T(8,128)}) custom-call(bf16[256,768]{1,0:T(8,128)(2,1)} %bitcast.10, bf16[1,768]{1,0:T(2,128)(2,1)} %broadcast_in_dim.20.refs_6_.refs_1_, ...), custom_call_target="tpu_custom_call", output_to_operand_aliasing={{0}: (29, {})} | custom-call | tf_op jit(solution)/shard_map/backward/pallas_call | solution.py:438
  231.5 0.0 copy-done.3
  231.5 0.0 copy-start
  231.5 2.3 copy-done
  233.8 0.0 copy-start.1
  233.8 1.1 copy-done.1
  235.0 0.0 copy-start.2
  235.0 1.1 copy-done.2
  236.1 0.0 copy-start.4
  236.1 0.8 copy-done.4
  236.9 5.0 %place.1 = (bf16[256,768]{1,0:T(8,128)(2,1)}, f32[256,768]{1,0:T(8,128)}, f32[256,768]{1,0:T(8,128)}, f32[768,768]{1,0:T(8,128)}, f32[192,3072]{1,0:T(8,128)}, /...) custom-call(bf16[3072,768]{1,0:T(8,128)(2,1)S(1)} %copy-done, ...), custom_call_target="tpu_custom_call" | custom-call | tf_op jit(solution)/shard_map/place/pallas_call | solution.py:1213
Async XLA Ops:
  52.5 179.0 %copy-start.3 = (bf16[256,768]{1,0:T(8,128)(2,1)S(1)}, bf16[256,768]{1,0:T(8,128)(2,1)}, u32[]{:S(2)}) copy-start(bf16[256,768]{1,0:T(8,128)(2,1)} %get-tuple-element.79.refs_2_) | copy-start | bytes 1179652
  231.5 2.3 copy-start
  233.8 1.1 copy-start.1
  235.0 1.1 copy-start.2
  236.1 0.8 copy-start.4

commit v3 on v2

--- a/solution.py
+++ b/solution.py
@@ -228,9 +228,9 @@
     r.xs[m.place] = r.x[...]
     r.es[m.place] = r.e[...]
 
-    gain_self = r.gain_self[...].astype(F32)
-    gain_cross = r.gain_cross[...].astype(F32)
-    gain_ffn = r.gain_ffn[...].astype(F32)
+    gain_self = r.gain_self[...].astype(F32).reshape(1, width)
+    gain_cross = r.gain_cross[...].astype(F32).reshape(1, width)
+    gain_ffn = r.gain_ffn[...].astype(F32).reshape(1, width)
 
     items = dims.items
     dec_starts, enc_starts = [0], [0]
@@ -256,13 +256,11 @@
 
     lax.fori_loop(0, places, masks, 0)
 
-    buckets = r.table.shape[0]
+    buckets = r.table.shape[1]
     terms = bucket_terms(buckets)
     last = lax.broadcasted_iota(jnp.int32, terms.shape, 0) == buckets - 1
     terms = terms - last.astype(F32)
-    r.near_bias[...] = lax.dot_general(
-        r.table[...], terms.astype(LOW), (((0,), (0,)), ((), ())), preferred_element_type=F32
-    )
+    r.near_bias[...] = dot(r.table[...], terms.astype(LOW))
 
     def self_block(place):
         rows = block(place, count)
@@ -462,10 +460,10 @@
         go=(a.out_grad[0], near),
         dec_len=(a.dec_lengths, scalars),
         enc_len=(a.enc_lengths, scalars),
-        table=(a.position_bias, near),
-        gain_self=(a.gain_self[None], near),
-        gain_cross=(a.gain_cross[None], near),
-        gain_ffn=(a.gain_ffn[None], near),
+        table=(a.position_bias.T, near),
+        gain_self=(a.gain_self, near),
+        gain_cross=(a.gain_cross, near),
+        gain_ffn=(a.gain_ffn, near),
         wk_hbm=(a.self_key, far),
         wv_hbm=(a.self_value, far),
         wq_hbm=(a.self_query, far),
@@ -545,24 +543,27 @@
 
 
 class Reducer:
-    LAG = 10
+    LAGS = (0, 3, 5, 7, 9, 11)
 
     def __init__(self, r, m, dims):
         self.r, self.m = r, m
         self.planes = dims.planes
+        self.line = dims.line
         self.piece = dims.piece
-        self.half_rows = self.piece * self.planes
-        self.chunk_rows = 2 * self.half_rows
+        self.chunk_rows = dims.chunk_rows
+        self.half_rows = dims.chunk_rows // 2
         self.chunks = dims.chunks
         self.ring = dims.ring
         self.plane, self.half = m.row // 2, lax.rem(m.row, 2)
         self.x_peer = (self.plane * 2 + 1 - self.half, m.place)
-        self.published = 0
-        self.done = 0
+        self.published = self.loaded = self.fed = self.moved = 0
 
     def z_peer(self, step):
         return (lax.rem(self.plane + step, self.planes) * 2 + self.half, self.m.place)
 
+    def plane_peer(self, plane):
+        return (plane * 2 + self.half, self.m.place)
+
     def peers(self):
         return [self.x_peer] + [self.z_peer(step) for step in range(1, self.planes)]
 
@@ -572,63 +573,100 @@
     def rows(self, index):
         return self.span(index * self.chunk_rows, self.chunk_rows)
 
-    def kept_rows(self, index, first=0, size=None):
-        slot = lax.rem(index, self.ring)
-        return self.span(slot * self.chunk_rows + first, size or self.chunk_rows)
+    def by_planes(self, index):
+        return lax.rem(index, 3) == 1
+
+    def route(self, index, first, other):
+        if not self.line:
+            first(index)
+            return
+        special = self.by_planes(index)
+
+        @pl.when(jnp.logical_not(special))
+        def _():
+            first(index)
+
+        @pl.when(special)
+        def _():
+            other(index)
+
+    def half_of(self, index, half):
+        return self.span(index * self.chunk_rows + half * self.half_rows, self.half_rows)
+
+    def packed(self, index):
+        return self.span(index * self.half_rows, self.half_rows)
+
+    def fresh_rows(self, index):
+        return self.span(lax.rem(index, self.ring) * self.chunk_rows, self.chunk_rows)
 
     def load(self, index):
         r = self.r
         return pltpu.make_async_copy(
             r.big.at[self.m.core, :, self.rows(index)],
-            r.kept.at[:, self.kept_rows(index)],
+            r.fresh.at[:, self.fresh_rows(index)],
             r.chunk_sem.at[index],
         )
 
     def core_copy(self, index):
         r, rows = self.r, self.rows(index)
         return send(
-            r.big.at[1 - self.m.core, :, rows], r.core_recv.at[:, rows], r.core_sem, (index,),
+            r.big.at[1 - self.m.core, :, rows], r.sums.at[:, rows], r.core_sem, (index,),
             self.m.core_peer,
         )
 
     def y_copy(self, index):
+        r, rows = self.r, self.rows(index)
+        return send(
+            r.sums.at[1 - self.m.side, rows], r.fin.at[rows], r.y_sem, (index,), self.m.y_peer
+        )
+
+    def x_copy(self, index):
         r = self.r
         return send(
-            r.kept.at[1 - self.m.side, self.kept_rows(index)], r.fin.at[self.rows(index)],
-            r.y_sem, (index,), self.m.y_peer,
-        )
-
-    def x_copy(self, index):
+            r.sums.at[self.m.side, self.half_of(index, 1 - self.half)],
+            r.x_recv.at[self.packed(index)],
+            r.x_sem, (index,), self.x_peer,
+        )
+
+    def in_copy(self, index, inner):
         r = self.r
-        other = self.kept_rows(index, (1 - self.half) * self.half_rows, self.half_rows)
         return send(
-            r.kept.at[self.m.side, other],
-            r.x_recv.at[self.span(index * self.half_rows, self.half_rows)],
-            r.x_sem, (index,), self.x_peer,
-        )
-
-    def z_first(self, which):
-        return self.half * self.half_rows + which * self.piece
+            r.sums.at[self.m.side, self.half_of(index, self.half)],
+            r.z_recv.at[0, self.packed(index)],
+            r.z_sem, (index, 0), self.plane_peer(inner),
+        )
+
+    def mid_copy(self, index):
+        r = self.r
+        return send(
+            r.sums.at[self.m.side, self.half_of(index, self.half)],
+            r.z_recv.at[1, self.packed(index)],
+            r.z_sem, (index, 1), self.plane_peer(3 - self.plane),
+        )
+
+    def out_copy(self, index, outer):
+        r, rows = self.r, self.half_of(index, self.half)
+        return send(r.fin.at[rows], r.fin.at[rows], r.gz_sem, (index, 0), self.plane_peer(outer))
+
+    def z_part(self, index, which):
+        first = index * self.chunk_rows + self.half * self.half_rows + which * self.piece
+        return self.span(first, self.piece)
 
     def z_copy(self, index, step):
         r = self.r
         target = lax.rem(self.plane + step, self.planes)
         return send(
-            r.kept.at[self.m.side, self.kept_rows(index, self.z_first(target), self.piece)],
+            r.sums.at[self.m.side, self.z_part(index, target)],
             r.z_recv.at[step - 1, self.span(index * self.piece, self.piece)],
             r.z_sem, (index, step - 1), self.z_peer(step),
         )
 
-    def own_rows(self, index):
-        return self.span(index * self.chunk_rows + self.z_first(self.plane), self.piece)
-
     def gz_copy(self, index, step):
-        r, rows = self.r, self.own_rows(index)
+        r, rows = self.r, self.z_part(index, self.plane)
         return send(r.fin.at[rows], r.fin.at[rows], r.gz_sem, (index, step - 1), self.z_peer(step))
 
     def gx_copy(self, index):
-        r = self.r
-        rows = self.span(index * self.chunk_rows + self.half * self.half_rows, self.half_rows)
+        r, rows = self.r, self.half_of(index, self.half)
         return send(r.fin.at[rows], r.fin.at[rows], r.gx_sem, (index,), self.x_peer)
 
     def publish(self, rows):
@@ -643,109 +681,260 @@
             return carry
 
         lax.fori_loop(self.published, last, begin, 0)
-        first_load = max(self.published, 0)
-        last_load = min(last, max(self.ring, self.freed() + self.ring))
-        lax.fori_loop(first_load, last_load, fetch, 0)
-        self.published = last
-        self.loaded = last_load
-
-    def freed(self):
-        return max(0, self.done - 6)
-
-    def tick(self, step):
-        r, m, chunks = self.r, self.m, self.chunks
-
-        @pl.when(step < chunks)
+        ahead = min(last, self.fed + self.ring)
+        lax.fori_loop(self.loaded, ahead, fetch, 0)
+        self.published, self.loaded = last, max(self.loaded, ahead)
+
+    def feed(self, index):
+        r = self.r
+        self.load(index).wait()
+        self.core_copy(index).wait()
+        rows, fresh = self.rows(index), self.fresh_rows(index)
+        for side in range(2):
+            r.sums[side, rows, :] = add_low(r.sums[side, rows, :], r.fresh[side, fresh, :])
+        self.route(
+            index, lambda at: self.y_copy(at).start(), lambda at: self.swap_copy(at).start()
+        )
+
+        @pl.when(index + self.ring < self.published)
         def _():
-            self.load(step).wait()
-            self.core_copy(step).wait()
-            rows, kept = self.rows(step), self.kept_rows(step)
-            for other in range(2):
-                r.kept[other, kept, :] = add_low(r.kept[other, kept, :], r.core_recv[other, rows, :])
-            self.y_copy(step).start()
-
-        @pl.when((step >= 2) & (step < chunks + 2))
+            self.load(index + self.ring).start()
+
+    def move(self, step):
+        stages = (
+            (self.after_y, self.after_swap),
+            (self.after_x, self.swapped_y),
+            (self.inward, self.swapped_x),
+            (self.middle, self.swapped_pair),
+            (self.outward, self.swapped_back),
+            (self.finish, self.swapped_finish),
+        )
+        for lag, stage in reversed(tuple(zip(self.LAGS, stages))):
+            index = step - lag
+
+            @pl.when((index >= 0) & (index < self.chunks))
+            def _():
+                self.route(index, *stage)
+
+
+    def parity(self):
+        return lax.rem(self.plane, 2)
+
+    def neighbour(self):
+        return self.plane_peer(self.plane + 1 - 2 * self.parity())
+
+    def quarter_of(self, index, half):
+        size = self.half_rows // 2
+        first = index * self.chunk_rows + self.parity() * self.half_rows + half * size
+        return self.span(first, size)
+
+    def packed_quarter(self, index, which):
+        size = self.half_rows // 2
+        return self.span(index * self.half_rows + which * size, size)
+
+    def swap_copy(self, index):
+        r = self.r
+        return send(
+            r.sums.at[:, self.half_of(index, 1 - self.parity())],
+            r.z_recv.at[:, self.packed(index)],
+            r.z_sem, (index, 0), self.neighbour(),
+        )
+
+    def swapped_y_copy(self, index):
+        r, rows = self.r, self.half_of(index, self.parity())
+        return send(
+            r.sums.at[1 - self.m.side, rows], r.fin.at[rows], r.y_sem, (index,), self.m.y_peer
+        )
+
+    def swapped_x_copy(self, index):
+        r = self.r
+        return send(
+            r.sums.at[self.m.side, self.quarter_of(index, 1 - self.half)],
+            r.x_recv.at[self.packed_quarter(index, 0)],
+            r.x_sem, (index,), self.x_peer,
+        )
+
+    def pair_copy(self, index):
+        r = self.r
+        return send(
+            r.sums.at[self.m.side, self.quarter_of(index, self.half)],
+            r.x_recv.at[self.packed_quarter(index, 1)],
+            r.z_sem, (index, 1), self.z_peer(2),
+        )
+
+    def swapped_gx_copy(self, index):
+        r, rows = self.r, self.quarter_of(index, self.half)
+        return send(r.fin.at[rows], r.fin.at[rows], r.gx_sem, (index,), self.x_peer)
+
+    def swapped_gz_copy(self, index):
+        r, rows = self.r, self.half_of(index, self.parity())
+        return send(r.fin.at[rows], r.fin.at[rows], r.gz_sem, (index, 0), self.neighbour())
+
+    def after_swap(self, index):
+        r = self.r
+        self.swap_copy(index).wait()
+        rows, packed = self.half_of(index, self.parity()), self.packed(index)
+        for side in range(2):
+            r.sums[side, rows, :] = add_low(r.sums[side, rows, :], r.z_recv[side, packed, :])
+        self.swapped_y_copy(index).start()
+
+    def swapped_y(self, index):
+        r, m = self.r, self.m
+        self.swapped_y_copy(index).wait()
+        rows = self.half_of(index, self.parity())
+        r.sums[m.side, rows, :] = add_low(r.sums[m.side, rows, :], r.fin[rows, :])
+        self.swapped_x_copy(index).start()
+
+    def swapped_x(self, index):
+        r, m = self.r, self.m
+        self.swapped_x_copy(index).wait()
+        rows = self.quarter_of(index, self.half)
+        arrived = r.x_recv[self.packed_quarter(index, 0), :]
+        r.sums[m.side, rows, :] = add_low(r.sums[m.side, rows, :], arrived)
+        self.pair_copy(index).start()
+
+    def swapped_pair(self, index):
+        r, m = self.r, self.m
+        self.pair_copy(index).wait()
+        rows = self.quarter_of(index, self.half)
+        arrived = r.x_recv[self.packed_quarter(index, 1), :]
+        r.fin[rows, :] = add_low(r.sums[m.side, rows, :], arrived)
+        self.swapped_gx_copy(index).start()
+
+    def swapped_back(self, index):
+        self.swapped_gx_copy(index).wait()
+        self.swapped_gz_copy(index).start()
+
+    def swapped_finish(self, index):
+        self.swapped_gz_copy(index).wait()
+
+    def after_y(self, index):
+        r, m = self.r, self.m
+        self.y_copy(index).wait()
+        rows = self.rows(index)
+        r.sums[m.side, rows, :] = add_low(r.sums[m.side, rows, :], r.fin[rows, :])
+        self.x_copy(index).start()
+
+    def after_x(self, index):
+        r, m = self.r, self.m
+        self.x_copy(index).wait()
+        rows = self.half_of(index, self.half)
+        r.sums[m.side, rows, :] = add_low(r.sums[m.side, rows, :], r.x_recv[self.packed(index), :])
+        if not self.line:
+            for step in range(1, self.planes):
+                self.z_copy(index, step).start()
+            return
+        for outer, inner in ((0, 1), (3, 2)):
+            @pl.when(self.plane == outer)
+            def _():
+                self.in_copy(index, inner).start()
+
+    def inward(self, index):
+        r, m = self.r, self.m
+        if not self.line:
+            return
+        for outer, inner in ((0, 1), (3, 2)):
+            @pl.when(self.plane == outer)
+            def _():
+                self.in_copy(index, inner).wait_send()
+
+        @pl.when((self.plane == 1) | (self.plane == 2))
         def _():
-            index = step - 2
-            self.y_copy(index).wait()
-            kept = self.kept_rows(index)
-            r.kept[m.side, kept, :] = add_low(r.kept[m.side, kept, :], r.fin[self.rows(index), :])
-            self.x_copy(index).start()
-
-        @pl.when((step >= 4) & (step < chunks + 4))
+            self.in_copy(index, self.plane).wait_recv()
+            rows = self.half_of(index, self.half)
+            arrived = r.z_recv[0, self.packed(index), :]
+            r.sums[m.side, rows, :] = add_low(r.sums[m.side, rows, :], arrived)
+            self.mid_copy(index).start()
+
+    def middle(self, index):
+        r, m = self.r, self.m
+        if not self.line:
+            part = self.z_part(index, self.plane)
+            total = r.sums[m.side, part, :].astype(F32)
+            for step in range(1, self.planes):
+                self.z_copy(index, step).wait()
+                arrived = r.z_recv[step - 1, self.span(index * self.piece, self.piece), :]
+                total = total + arrived.astype(F32)
+            r.fin[part, :] = total.astype(LOW)
+            for step in range(1, self.planes):
+                self.gz_copy(index, step).start()
+            return
+
+        @pl.when((self.plane == 1) | (self.plane == 2))
         def _():
-            index = step - 4
-            self.x_copy(index).wait()
-            kept = self.kept_rows(index, self.half * self.half_rows, self.half_rows)
-            arrived = r.x_recv[self.span(index * self.half_rows, self.half_rows), :]
-            r.kept[m.side, kept, :] = add_low(r.kept[m.side, kept, :], arrived)
-            for plane in range(1, self.planes):
-                self.z_copy(index, plane).start()
-
-        @pl.when((step >= 6) & (step < chunks + 6))
-        def _():
-            index = step - 6
-            kept = self.kept_rows(index, self.z_first(self.plane), self.piece)
-            total = r.kept[m.side, kept, :].astype(F32)
-            for plane in range(1, self.planes):
-                self.z_copy(index, plane).wait()
-                arrived = r.z_recv[plane - 1, self.span(index * self.piece, self.piece), :]
-                total = total + arrived.astype(F32)
-            r.fin[self.own_rows(index), :] = total.astype(LOW)
-            for plane in range(1, self.planes):
-                self.gz_copy(index, plane).start()
-
-        @pl.when((step >= 8) & (step < chunks + 8))
-        def _():
-            index = step - 8
-            for plane in range(1, self.planes):
-                self.gz_copy(index, plane).wait()
+            self.mid_copy(index).wait()
+            rows = self.half_of(index, self.half)
+            arrived = r.z_recv[1, self.packed(index), :]
+            r.fin[rows, :] = add_low(r.sums[m.side, rows, :], arrived)
+            for outer, inner in ((0, 1), (3, 2)):
+                @pl.when(self.plane == inner)
+                def _():
+                    self.out_copy(index, outer).start()
             self.gx_copy(index).start()
 
-        @pl.when(step >= 10)
-        def _():
-            self.gx_copy(step - 10).wait()
-
-    def fetch_next(self, step, limit):
-        index = step - 6 + self.ring
-
-        @pl.when((step >= 6) & (index >= self.loaded) & (index < limit))
-        def _():
-            self.load(index).start()
-
-    def run(self, ticks):
-        first = self.done
-
-        def one(step, carry):
-            self.tick(step)
-            self.fetch_next(step, self.published)
+    def outward(self, index):
+        if not self.line:
+            for step in range(1, self.planes):
+                self.gz_copy(index, step).wait()
+            self.gx_copy(index).start()
+            return
+        for outer, inner in ((0, 1), (3, 2)):
+            @pl.when(self.plane == inner)
+            def _():
+                self.out_copy(index, outer).wait_send()
+
+            @pl.when(self.plane == outer)
+            def _():
+                self.out_copy(index, inner).wait_recv()
+                self.gx_copy(index).start()
+
+    def finish(self, index):
+        self.gx_copy(index).wait()
+
+    def run(self, feeds, moves):
+        loops = max(1, feeds, moves)
+        one, after = self.beside(loops, feeds, moves)
+
+        def body(index, carry):
+            one(index)
             return carry
 
-        lax.fori_loop(first, first + ticks, one, 0)
-        self.advance(ticks)
-
-    def advance(self, ticks):
-        self.done += ticks
-        self.loaded = max(self.loaded, min(self.published, self.freed() + self.ring))
-
-    def ready(self):
-        if self.published == self.chunks:
-            return self.chunks + self.LAG - self.done
-        return self.published - self.done
-
-    def beside(self, loops):
-        first, ticks = self.done, min(loops, self.ready())
+        lax.fori_loop(0, loops, body, 0)
+        after()
+
+    def beside(self, loops, feeds, moves):
+        feeds = max(0, min(feeds, self.published - self.fed))
+        fed = self.fed + feeds
+        limit = self.chunks + self.LAGS[-1] if fed == self.chunks else fed
+        moves = max(0, min(moves, limit - self.moved))
+        first_feed, first_move = self.fed, self.moved
+
+        each = -(-feeds // loops)
 
         def one(index):
-            @pl.when(index < ticks)
-            def _():
-                self.tick(first + index)
-                self.fetch_next(first + index, self.published)
+            if feeds > 0:
+                def feed(step, carry):
+                    self.feed(first_feed + step)
+                    return carry
+
+                lax.fori_loop(
+                    jnp.minimum(index * each, feeds), jnp.minimum((index + 1) * each, feeds), feed, 0
+                )
+            if moves > 0:
+                def move(step, carry):
+                    self.move(first_move + step)
+                    return carry
+
+                lax.fori_loop(index * moves // loops, (index + 1) * moves // loops, move, 0)
 
         def after():
-            self.advance(ticks)
+            self.fed, self.moved = fed, first_move + moves
+            self.loaded = max(self.loaded, min(self.published, self.fed + self.ring))
 
         return one, after
+
+    def left(self):
+        return self.chunks + self.LAGS[-1] - self.moved
 
 
 def attend_back(pair, r, count, keys, keys_t, values, queries_t, masses, context_t, grad_t, probs, place, places):
@@ -860,8 +1049,8 @@
     m.greet([m.core_peer, m.y_peer] + engine.peers())
     engine.publish(2 * width)
 
-    gain_self = r.gain_self[...].astype(F32)
-    gain_cross = r.gain_cross[...].astype(F32)
+    gain_self = r.gain_self[...].astype(F32).reshape(1, width)
+    gain_cross = r.gain_cross[...].astype(F32).reshape(1, width)
     staged = {}
 
     def unit_copy(unit):
@@ -892,8 +1081,8 @@
 
         lax.fori_loop(0, places, one, 0)
 
-    def attend(src, queries_t, masses, context_t, grad_t, place):
-        tick, after = engine.beside(pairs)
+    def attend(src, queries_t, masses, context_t, grad_t, place, feeds, moves):
+        beside, after = engine.beside(pairs, feeds, moves)
 
         def one(pair, carry):
             probs_copy(src, pair).wait()
@@ -906,7 +1095,7 @@
             def _():
                 probs_copy(src, pair + 2).start()
 
-            tick(pair)
+            beside(pair)
             return carry
 
         lax.fori_loop(0, pairs, one, 0)
@@ -934,17 +1123,19 @@
     loads.cwo.wait()
     r.grad_t[...] = dot_nt(r.wo[...], head_grad).astype(LOW)
     loads.wo = load(r.wo_hbm, r.wo)
+    engine.run(2, 0)
     give(0, r.ccontext_t[...].astype(LOW), head_grad)
     loads.ckeys.wait()
     turn(r.keys, r.keys_t)
     loads.cvalues.wait()
-    attend(r.cross_probs, r.cqueries_t, r.cross_masses, r.ccontext_t, r.grad_t, None)
+    attend(r.cross_probs, r.cqueries_t, r.cross_masses, r.ccontext_t, r.grad_t, None, 4, 3)
     copies = exchange(0, r.key_recv.at[0], r.value_recv.at[0])
     loads.keys = load(r.keys_hbm, r.keys)
     loads.values = load(r.values_hbm, r.values)
     probs_copy(r.self_probs, 0).start()
     probs_copy(r.self_probs, 1).start()
     query_grad = jnp.transpose(r.query_grad_t[...])
+    engine.run(0, 1)
     loads.cwq.wait()
     normed_grad = dot_nt(query_grad, r.wq[...])
     loads.wq = load(r.wq_hbm, r.wq)
@@ -952,6 +1143,7 @@
     first_part, gain_cross_grad = norm_back(r.enc_grad[...], gain_cross, normed_grad)
     r.dec_grad[...] += first_part
     give(1, jnp.transpose(r.a2[...]), query_grad)
+    engine.run(0, 1)
     loads.es0.wait()
     loads.es1.wait()
     for side in range(2):
@@ -973,6 +1165,7 @@
     give(2, r.group_t[...], key_grad)
     give(3, r.group_t[...], value_grad)
     settle(3 * width)
+    engine.run(3, 2)
 
     first_grad = r.dec_grad[...]
     head_grad = first_grad.astype(LOW)
@@ -991,9 +1184,10 @@
 
     lax.fori_loop(m.place + 1, places, clear, 0)
     r.by_distance[...] = jnp.zeros_like(r.by_distance)
-    attend(r.self_probs, r.queries_t, r.self_masses, r.context_t, r.grad_t, m.place)
+    attend(r.self_probs, r.queries_t, r.self_masses, r.context_t, r.grad_t, m.place, 6, 6)
     copies = exchange(2, r.key_recv.at[1], r.value_recv.at[1])
     query_grad = jnp.transpose(r.query_grad_t[...])
+    engine.run(0, 1)
     loads.wq.wait()
     normed_grad = dot_nt(query_grad, r.wq[...])
     loads.a10.wait()
@@ -1001,6 +1195,7 @@
     for side in range(2):
         r.group_t[:, side * count : (side + 1) * count] = jnp.transpose(r.group[side])
     give(5, jnp.transpose(r.group[m.side]), query_grad)
+    engine.run(0, 1)
     for copy in copies:
         copy.wait()
     key_grad = chip_sum(r.key_grad, r.key_recv.at[1])
@@ -1016,6 +1211,7 @@
     give(6, r.group_t[...], key_grad)
     give(7, r.group_t[...], value_grad)
     settle(4 * width)
+    engine.run(4, 2)
     dec_copy.wait()
     normed_grad = normed_grad + r.partial_recv[1].astype(F32)
     state_part, gain_self_grad = norm_back(r.x[...].astype(F32), gain_self, normed_grad)
@@ -1038,6 +1234,7 @@
     for slot, peer in enumerate((m.core_peer, m.y_peer, engine.x_peer)):
         copy = send(r.tiny.at[slot], r.tiny_recv.at[slot], r.tiny_sem, (slot,), peer)
         copy.start()
+        engine.run(1, 1)
         copy.wait()
         r.tiny[slot + 1] = r.tiny[slot] + r.tiny_recv[slot]
     copies = []
@@ -1047,13 +1244,14 @@
         )
         copy.start()
         copies.append(copy)
+    engine.run(1, 1)
     for copy in copies:
         copy.wait()
     total = r.tiny[3]
     for step in range(1, dims.planes):
         total = total + r.tiny_recv[2 + step]
     r.small[...] = total
-    engine.run(engine.ready())
+    engine.run(engine.chunks, engine.left())
 
 
 def run_backward(dims, a, f):
@@ -1064,8 +1262,8 @@
     own = (count, width)
     inputs = dict(
         x=(a.dec_states[0], near),
-        gain_self=(a.gain_self[None], near),
-        gain_cross=(a.gain_cross[None], near),
+        gain_self=(a.gain_self, near),
+        gain_cross=(a.gain_cross, near),
         first_hbm=(f.first, far),
         second_hbm=(f.second_grad, far),
         gain_ffn_grad=(f.gain_ffn_grad, near),
@@ -1103,7 +1301,6 @@
     )
     dma = pltpu.SemaphoreType.DMA
     rows = 4 * width
-    chunk_rows = 2 * planes * piece
     scratch = dict(
         wo=pltpu.VMEM(square, LOW),
         wq=pltpu.VMEM(square, LOW),
@@ -1126,10 +1323,12 @@
         before=pltpu.VMEM((NEAR, 2 * count), F32),
         by_distance=pltpu.VMEM((128, 2 * NEAR), F32),
         stage=pltpu.VMEM((2, 2, 2, width // dims.places, width), LOW),
-        kept=pltpu.VMEM((2, dims.ring * chunk_rows, width), LOW),
-        core_recv=pltpu.VMEM((2, rows, width), LOW),
+        fresh=pltpu.VMEM((2, dims.ring * dims.chunk_rows, width), LOW),
+        sums=pltpu.VMEM((2, rows, width), LOW),
         x_recv=pltpu.VMEM((rows // 2, width), LOW),
-        z_recv=pltpu.VMEM((planes - 1, chunks * piece, width), LOW),
+        z_recv=pltpu.VMEM(
+            (2, rows // 2, width) if dims.line else (planes - 1, chunks * piece, width), LOW
+        ),
         tiny=pltpu.VMEM((4, 16, width), F32),
         tiny_recv=pltpu.VMEM((2 + planes, 16, width), F32),
         load_sem=dma((18,)),
@@ -1155,20 +1354,48 @@
     r = SimpleNamespace(**dict(zip(names, refs)))
     width, fan = dims.width, dims.fan
     own = width // dims.places
-    r.ffn_out_grad[...] = r.fin[:width].astype(F32)
-    for index in range(fan):
-        first = width + index * own
-        r.ffn_in_grad[:, index * width : (index + 1) * width] = r.fin[first : first + own].astype(F32)
+    passed = (
+        (r.layer_in, r.layer_held, r.layer),
+        (r.dec_in, r.dec_held, r.dec),
+        (r.enc_in, r.enc_held, r.enc),
+    )
+    inward = [
+        pltpu.make_async_copy(src, held, r.pass_sem.at[0, slot])
+        for slot, (src, held, _) in enumerate(passed)
+    ]
+    copies = [
+        pltpu.make_async_copy(held, dst, r.pass_sem.at[1, slot])
+        for slot, (_, held, dst) in enumerate(passed)
+    ]
+    groups = 4 * width // own
+    loads, stores = [], []
+    for index in range(4):
+        rows = pl.ds(index * width, width)
+        loads.append(pltpu.make_async_copy(r.fin.at[rows], r.low.at[rows], r.load_sem.at[index]))
+        loads[-1].start()
+    for copy in inward:
+        copy.start()
     units = (
         r.cross_output, r.cross_query, r.cross_key, r.cross_value,
         r.self_output, r.self_query, r.self_key, r.self_value,
     )
-    for index, grad in enumerate(units):
-        first = 2 * width + index * own
-        grad[...] = r.fin[first : first + own].astype(F32)
-    r.layer[...] = r.layer_in[...]
-    r.dec[...] = r.dec_in[...]
-    r.enc[...] = r.enc_in[...]
+    for index in range(groups):
+        if index % (groups // 4) == 0:
+            loads[index // (groups // 4)].wait()
+        rows = pl.ds(index * own, own)
+        r.wide[rows, :] = r.low[rows, :].astype(F32)
+        if index < fan:
+            dst = r.ffn_out.at[rows]
+        elif index < 2 * fan:
+            dst = r.ffn_in.at[:, pl.ds((index - fan) * width, width)]
+        else:
+            dst = units[index - 2 * fan]
+        copy = pltpu.make_async_copy(r.wide.at[rows], dst, r.store_sem.at[index])
+        copy.start()
+        stores.append(copy)
+    for arrival, copy in zip(inward, copies):
+        arrival.wait()
+        copy.start()
     at = lax.axis_index("seq")
     part = dims.buckets // dims.places
     for place in range(dims.places):
@@ -1177,25 +1404,28 @@
             for index, grad in enumerate((r.gain_self, r.gain_cross, r.gain_ffn)):
                 grad[...] = r.small[index : index + 1, place * own : (place + 1) * own]
             r.table_grad[...] = r.small[8 : 8 + part, 128 * place : 128 * place + dims.heads]
+    for copy in stores + copies:
+        copy.wait()
 
 
 def run_place(dims, f, b):
-    near = pltpu.VMEM
+    near, far = pltpu.VMEM, pl.ANY
     width, own = dims.width, dims.width // dims.places
-    square, gain = ((own, width), F32, near), ((1, own), F32, near)
+    square, gain = ((own, width), F32, far), ((1, own), F32, near)
+    rows = 4 * width
     inputs = dict(
-        fin=(b.fin, near),
+        fin=(b.fin, far),
         small=(b.small, near),
-        layer_in=(f.layer_out, near),
-        dec_in=(b.dec_grad, near),
-        enc_in=(b.enc_grad, near),
+        layer_in=(f.layer_out, far),
+        dec_in=(b.dec_grad, far),
+        enc_in=(b.enc_grad, far),
     )
     outputs = dict(
-        layer=(f.layer_out.shape, LOW, near),
-        dec=(b.dec_grad.shape, F32, near),
-        enc=(b.enc_grad.shape, F32, near),
-        ffn_out_grad=((width, width), F32, near),
-        ffn_in_grad=((own, dims.fan * width), F32, near),
+        layer=(f.layer_out.shape, LOW, far),
+        dec=(b.dec_grad.shape, F32, far),
+        enc=(b.enc_grad.shape, F32, far),
+        ffn_out=((width, width), F32, far),
+        ffn_in=((own, dims.fan * width), F32, far),
         cross_output=square,
         cross_query=square,
         cross_key=square,
@@ -1209,13 +1439,24 @@
         gain_ffn=gain,
         table_grad=((dims.buckets // dims.places, dims.heads), F32, near),
     )
-    names = (*inputs, *outputs)
+    scratch = dict(
+        low=pltpu.VMEM((rows, width), LOW),
+        wide=pltpu.VMEM((rows, width), F32),
+        layer_held=pltpu.VMEM(f.layer_out.shape, LOW),
+        dec_held=pltpu.VMEM(b.dec_grad.shape, F32),
+        enc_held=pltpu.VMEM(b.enc_grad.shape, F32),
+        pass_sem=pltpu.SemaphoreType.DMA((2, 3)),
+        load_sem=pltpu.SemaphoreType.DMA((4,)),
+        store_sem=pltpu.SemaphoreType.DMA((rows // own,)),
+    )
+    names = (*inputs, *outputs, *scratch)
     results = pl.pallas_call(
         lambda *refs: place_kernel(names, dims, *refs),
         out_shape=tuple(jax.ShapeDtypeStruct(shape, kind) for shape, kind, _ in outputs.values()),
         in_specs=[pl.BlockSpec(memory_space=space) for _, space in inputs.values()],
         out_specs=tuple(pl.BlockSpec(memory_space=space) for _, _, space in outputs.values()),
-        compiler_params=pltpu.CompilerParams(vmem_limit_bytes=40 * 2**20),
+        scratch_shapes=list(scratch.values()),
+        compiler_params=pltpu.CompilerParams(vmem_limit_bytes=60 * 2**20),
         name="place",
     )(*(array for array, _ in inputs.values()))
     return SimpleNamespace(**dict(zip(outputs, results)))
@@ -1266,7 +1507,9 @@
     count, width = a.dec_states.shape[1:]
     buckets, heads = a.position_bias.shape
     planes, piece = lax.axis_size("dp") // 2, 16
-    chunks = 4 * width // (2 * planes * piece)
+    line = planes == 4
+    chunk_rows = 128 if line else 2 * planes * piece
+    chunks = 4 * width // chunk_rows
     dims = SimpleNamespace(
         count=count,
         width=width,
@@ -1280,7 +1523,9 @@
         planes=planes,
         piece=piece,
         chunks=chunks,
-        ring=min(chunks, 12),
+        ring=4 if line else 1,
+        line=line,
+        chunk_rows=chunk_rows,
     )
     f = run_forward(dims, a)
     b = run_backward(dims, a, f)
@@ -1297,8 +1542,8 @@
         o.cross_key,
         o.cross_value,
         o.cross_output,
-        o.ffn_in_grad,
-        o.ffn_out_grad,
+        o.ffn_in,
+        o.ffn_out,
         o.gain_self[0],
         o.gain_cross[0],
         o.gain_ffn[0],

time: 242 us -> 213 us (0.88)
  Pallas kernels: 231 us -> 212 us
  local copies, waits for them, and re-layouts: 10.6 us -> 0 us
    pallas_call x2, Pallas kernels: 226 us -> 204 us  [call(): pl.pallas_call(functools.partial(kernel, names), out_shape=tuple((jax.Sha...]
    unnamed x11 -> x0, local copies, waits for them, and re-layouts: 6.77 us -> none
    broadcast_in_dim x3 -> x0, local copies, waits for them, and re-layouts: 3.79 us -> none  [the longest x1 1.26 us: run_backward(): a.gain_self[None]]
    pallas_call x1, Pallas kernels: 4.95 us -> 7.41 us  [run_place(): pl.pallas_call(lambda *refs: place_kernel(names, dims, *refs), out_shape=...]
where the time goes in v3:
time: 213 us
  Pallas kernels  212 us (100%)
    pallas_call x2, Pallas kernels, call(): pl.pallas_call(functools.partial(kernel, names), out_shape=tuple((jax.Sha...  204 us
    pallas_call x1, Pallas kernels, run_place(): pl.pallas_call(lambda *refs: place_kernel(names, dims, *refs), out_shape=...  7.41 us

profile of v3, /device:TPU:0, one launch (start us, length us, event | category | flops | bytes accessed | tf_op | source)
XLA Modules:
  0.0 212.7 jit_solution(6651917392998518251)
XLA Ops:
  0.7 47.0 %forward.1 = (bf16[256,768]{1,0:T(8,128)(2,1)}, f32[256,768]{1,0:T(8,128)}, f32[256,768]{1,0:T(8,128)}, f32[1,768]{1,0:T(1,128)}, bf16[768,256]{1,0:T(8,128)(2,1...) custom-call(bf16[256,768]{1,0:T(8,128)(2,1)} %bitcast.10, ...), custom_call_target="tpu_custom_call" | custom-call | tf_op jit(solution)/shard_map/forward/pallas_call | solution.py:436
  47.6 157.4 %backward.1 = (bf16[2,2,3072,768]{3,2,1,0:T(8,128)(2,1)}, bf16[3072,768]{1,0:T(8,128)(2,1)}, f32[256,768]{1,0:T(8,128)}, f32[256,768]{1,0:T(8,128)}, f32[16,768]{1,0:T(8,128)}) custom-call(bf16[256,768]{1,0:T(8,128)(2,1)} %bitcast.11, bf16[768]{0:T(1024)(128)(2,1)} %refs_1_.1, bf16[768]{0:T(1024)(128)(2,1)} %refs_2_.1, ...), custom_call_target="tpu_custom_call", output_to_operand_aliasing={{0}: (29, {})} | custom-call | tf_op jit(solution)/shard_map/backward/pallas_call | solution.py:436
  205.1 7.4 %place.1 = (bf16[256,768]{1,0:T(8,128)(2,1)}, f32[256,768]{1,0:T(8,128)}, f32[256,768]{1,0:T(8,128)}, f32[768,768]{1,0:T(8,128)}, f32[192,3072]{1,0:T(8,128)}, /...) custom-call(bf16[3072,768]{1,0:T(8,128)(2,1)} %get-tuple-element.77., ...), custom_call_target="tpu_custom_call" | custom-call | tf_op jit(solution)/shard_map/place/pallas_call | solution.py:1453
